TPU v7x, 128 devices: a whole 4x4x4 slice. The times are simulated.
128 devices in a mesh: pipe: 2 (over z_hi), dp: 16 (over z_lo, y, core), tensor: 4 (over x).
Axes of the slice: x: 4, y: 4, z: 4 (z_hi: 2, z_lo: 2; z = z_hi * 2 + z_lo), core: 2. Of those that a mesh axis runs over, the one named last changes fastest.
Arguments:
- inputs: bfloat16 [2, 4096, 1024], P(None, ('dp', 'tensor')), may hold values from -6 to 6
- cotangent: bfloat16 [2, 4096, 1024], P(None, ('dp', 'tensor')), may hold values from -16 to 16
- doc_lengths: int32 [2, 16, 4], P(None, 'dp'), may hold values from 1 to 256, as said below
- routes: int32 [2, 2, 4096, 8], P('pipe', None, 'dp'), may hold values from 0 to 15, all different within a row; in each aligned block of 256 rows (0 to 255, 256 to 511, ..., all dimensions but the last counted through in order) at most 160 rows name the same one
- norm_attn: bfloat16 [2, 1024], P('pipe', ('dp', 'tensor')), may hold values from 0.5 to 1.5
- w_query: bfloat16 [2, 1024, 1024], P('pipe', 'dp', 'tensor'), may hold values from -0.1875 to 0.1875
- w_key: bfloat16 [2, 1024, 512], P('pipe', 'dp', 'tensor'), may hold values from -0.1875 to 0.1875
- w_value: bfloat16 [2, 1024, 512], P('pipe', 'dp', 'tensor'), may hold values from -0.1875 to 0.1875
- w_out: bfloat16 [2, 1024, 1024], P('pipe', 'tensor', 'dp'), may hold values from -0.75 to 0.75
- w_router: bfloat16 [2, 1024, 16], P('pipe', ('dp', 'tensor')), may hold values from -0.09375 to 0.09375
- norm_ffn: bfloat16 [2, 1024], P('pipe', ('dp', 'tensor')), may hold values from 0.5 to 1.5
- w_gate: bfloat16 [2, 16, 1024, 512], P('pipe', None, 'dp', 'tensor'), may hold values from -0.1875 to 0.1875
- w_up: bfloat16 [2, 16, 1024, 512], P('pipe', None, 'dp', 'tensor'), may hold values from -0.1875 to 0.1875
- w_down: bfloat16 [2, 16, 512, 1024], P('pipe', None, 'tensor', 'dp'), may hold values from -0.75 to 0.75
Outputs:
- section_out: bfloat16 [2, 2, 4096, 1024], P('pipe', None, ('dp', 'tensor'))
- input_grad: float32 [2, 2, 4096, 1024], P('pipe', None, ('dp', 'tensor'))
- grad_norm_attn: float32 [2, 1024], P('pipe', ('dp', 'tensor'))
- grad_query: float32 [2, 1024, 1024], P('pipe', 'dp', 'tensor')
- grad_key: float32 [2, 1024, 512], P('pipe', 'dp', 'tensor')
- grad_value: float32 [2, 1024, 512], P('pipe', 'dp', 'tensor')
- grad_out: float32 [2, 1024, 1024], P('pipe', 'tensor', 'dp')
- grad_router: float32 [2, 1024, 16], P('pipe', ('dp', 'tensor'))
- grad_norm_ffn: float32 [2, 1024], P('pipe', ('dp', 'tensor'))
- grad_gate: float32 [2, 16, 1024, 512], P('pipe', None, 'dp', 'tensor')
- grad_up: float32 [2, 16, 1024, 512], P('pipe', None, 'dp', 'tensor')
- grad_down: float32 [2, 16, 512, 1024], P('pipe', None, 'tensor', 'dp')
Inputs may be any that keep to these rules, and one draw needn't show every extreme that they name: `doc_lengths`: each row holds 4 lengths that sum to 256; one of these documents, at a place drawn from the seed, holds tokens of every index of tensor. `routes`: in each block of 256 consecutive rows (one section, one micro-batch, one pack) no expert is named more than 160 times, and in some blocks one expert is named exactly 160 times.
All inputs are finite; a program needn't handle non-finite values.
Results may differ from a plain program's by a relative error of at most 0.035.
Values may be sent and summed in bfloat16 or wider, within the bound.
No kernel may reach another device: no remote copies, remote signals or barrier semaphores. Data moves between devices by JAX's collectives and lax.ppermute only.
A program may use at most 192 MiB of HBM per device.

v0:
```python
import math

import jax
import jax.numpy as jnp
from jax import lax
from jax.sharding import PartitionSpec as P

HD = 64
E = 16
TOP = 8


EPSILON = 1e-06
MASKED = -1000000000.0


def shifted(array, axis, by):
    peers = lax.axis_size(axis)
    pairs = [(i, i + by) for i in range(peers) if 0 <= i + by < peers]
    return lax.ppermute(array, axis, pairs)


def rope_tables(position, head_width):
    half_width = head_width // 2
    freq_table = jnp.exp(
        jnp.arange(half_width, dtype=jnp.float32) * (-2.0 * math.log(10000.0) / head_width)
    )
    angle_table = position.astype(jnp.float32)[:, None] * freq_table[None, :]
    return (jnp.cos(angle_table), jnp.sin(angle_table))


def rotate(values, cosine_table, sine_table):
    half_width = values.shape[-1] // 2
    first_half = values[..., :half_width]
    second_half = values[..., half_width:]
    cosine_rows = cosine_table[:, None, :]
    sine_rows = sine_table[:, None, :]
    return jnp.concatenate(
        [
            first_half * cosine_rows - second_half * sine_rows,
            second_half * cosine_rows + first_half * sine_rows,
        ],
        axis=-1,
    )


def doc_layout(lengths, row_count):
    doc_ends = jnp.cumsum(lengths)
    doc_starts = doc_ends - lengths
    row_index = jnp.arange(row_count, dtype=jnp.int32)
    inside = row_index[:, None] >= doc_starts[None, :]
    segment = jnp.sum(inside.astype(jnp.int32), axis=1)
    position = row_index - jnp.max(jnp.where(inside, doc_starts[None, :], 0), axis=1)
    return (segment, position)


def slot_tables(chosen_ids, capacity):
    flat_ids = chosen_ids.reshape(-1)
    expert_ids = jnp.arange(E, dtype=jnp.int32)
    onehot = (flat_ids[:, None] == expert_ids[None, :]).astype(jnp.int32)
    running = jnp.cumsum(onehot, axis=0)
    rank_in = jnp.sum(running * onehot, axis=1) - 1
    slot_of = flat_ids * capacity + rank_in
    token_of = jnp.arange(flat_ids.shape[0], dtype=jnp.int32) // chosen_ids.shape[1]
    source = jnp.full((E * capacity,), chosen_ids.shape[0], jnp.int32).at[slot_of].set(token_of)
    return (slot_of, source)


def expert_rows(full_rows, source, capacity):
    padded = jnp.concatenate(
        [full_rows, jnp.zeros((1, full_rows.shape[1]), full_rows.dtype)], axis=0
    )
    return padded[source].reshape(E, capacity, full_rows.shape[1])


def rms_scale(values):
    return lax.rsqrt(jnp.mean(values * values, axis=-1, keepdims=True) + EPSILON)


def norm_back(values, scale_rows, gain, grad_normed):
    weighted = grad_normed * gain
    grad_values = scale_rows * weighted - values * scale_rows**3 * jnp.mean(
        weighted * values, axis=-1, keepdims=True
    )
    grad_gain = jnp.sum(grad_normed * values * scale_rows, axis=0)
    return (grad_values, grad_gain)


def spread(shard_rows):
    return lax.all_gather(shard_rows, "tensor", axis=0, tiled=True)


def collect(partial_rows):
    return lax.psum_scatter(
        partial_rows.astype(jnp.bfloat16), "tensor", scatter_dimension=0, tiled=True
    ).astype(jnp.float32)


def attention_scores(query_grouped, key_rows, visible):
    raw_scores = jnp.einsum(
        "tkgd,skd->kgts", query_grouped, key_rows, preferred_element_type=jnp.float32
    ) * HD ** (-0.5)
    return jnp.where(visible[None, None], raw_scores, MASKED)


def expert_grads_of(terms):
    expert_in, grad_gate_pre, grad_up_pre, activated, grad_expert = terms
    grad_weight_gate = jnp.einsum(
        "ecd,ecf->edf", expert_in, grad_gate_pre, preferred_element_type=jnp.float32
    )
    grad_weight_up = jnp.einsum(
        "ecd,ecf->edf", expert_in, grad_up_pre, preferred_element_type=jnp.float32
    )
    grad_weight_down = jnp.einsum(
        "ecf,ecd->efd", activated, grad_expert, preferred_element_type=jnp.float32
    )
    return (grad_weight_gate, grad_weight_up, grad_weight_down)


def slot_count(group_rows):
    return group_rows * TOP * 5 // (4 * E)


def layer_forward(entering, weights, smalls, chosen_ids, segment, position):
    weight_query, weight_key, weight_value, weight_out, weight_gate, weight_up, weight_down = (
        weights
    )
    weight_router, gain_attn, gain_ffn = smalls
    heads_query = weight_query.shape[1] // HD
    heads_kv = weight_key.shape[1] // HD
    scale_attn = rms_scale(entering)
    normed_attn = (entering * scale_attn * gain_attn).astype(jnp.bfloat16)
    full_attn = spread(normed_attn)
    group_rows = full_attn.shape[0]
    cosine_table, sine_table = rope_tables(position, HD)
    query_lin = jnp.dot(full_attn, weight_query, preferred_element_type=jnp.float32).reshape(
        group_rows, heads_query, HD
    )
    key_lin = jnp.dot(full_attn, weight_key, preferred_element_type=jnp.float32).reshape(
        group_rows, heads_kv, HD
    )
    query_rows = rotate(query_lin, cosine_table, sine_table).astype(jnp.bfloat16)
    key_rows = rotate(key_lin, cosine_table, sine_table).astype(jnp.bfloat16)
    value_rows = (
        jnp.dot(full_attn, weight_value, preferred_element_type=jnp.float32)
        .astype(jnp.bfloat16)
        .reshape(group_rows, heads_kv, HD)
    )
    query_grouped = query_rows.reshape(group_rows, heads_kv, heads_query // heads_kv, HD)
    row_index = jnp.arange(group_rows, dtype=jnp.int32)
    visible = (segment[:, None] == segment[None, :]) & (row_index[None, :] <= row_index[:, None])
    scores = attention_scores(query_grouped, key_rows, visible)
    score_peak = jnp.max(scores, axis=-1, keepdims=True)
    log_total = score_peak + jnp.log(jnp.sum(jnp.exp(scores - score_peak), axis=-1, keepdims=True))
    soft_low = jnp.exp(scores - log_total).astype(jnp.bfloat16)
    mixed = jnp.einsum("kgts,skd->tkgd", soft_low, value_rows, preferred_element_type=jnp.float32)
    mixed = mixed.reshape(group_rows, heads_query * HD).astype(jnp.bfloat16)
    hidden = entering + collect(jnp.dot(mixed, weight_out, preferred_element_type=jnp.float32))
    scale_ffn = rms_scale(hidden)
    normed_ffn = (hidden * scale_ffn * gain_ffn).astype(jnp.bfloat16)
    full_ffn = spread(normed_ffn)
    logits = jnp.dot(full_ffn, weight_router, preferred_element_type=jnp.float32)
    picked = chosen_ids[:, :, None] == jnp.arange(E, dtype=jnp.int32)[None, None, :]
    gate_values = jax.nn.softmax(
        jnp.sum(jnp.where(picked, logits[:, None, :], 0.0), axis=-1), axis=-1
    )
    capacity = slot_count(group_rows)
    slot_of, source = slot_tables(chosen_ids, capacity)
    expert_in = expert_rows(full_ffn, source, capacity)
    gate_pre = jnp.einsum(
        "ecd,edf->ecf", expert_in, weight_gate, preferred_element_type=jnp.float32
    )
    up_pre = jnp.einsum("ecd,edf->ecf", expert_in, weight_up, preferred_element_type=jnp.float32)
    activated = (jax.nn.silu(gate_pre) * up_pre).astype(jnp.bfloat16)
    expert_out = jnp.einsum(
        "ecf,efd->ecd", activated, weight_down, preferred_element_type=jnp.float32
    )
    per_token = expert_out.reshape(E * capacity, -1)[slot_of].reshape(group_rows, TOP, -1)
    result = hidden + collect(jnp.sum(gate_values[:, :, None] * per_token, axis=1))
    kept = (
        scale_attn,
        full_attn,
        query_grouped,
        key_rows,
        value_rows,
        visible,
        log_total,
        mixed,
        hidden,
        scale_ffn,
        normed_ffn,
        full_ffn,
        picked,
        gate_values,
        slot_of,
        source,
        gate_pre,
        up_pre,
        activated,
        cosine_table,
        sine_table,
    )
    return (result, kept)


def layer_backward(entering, grad_result, weights, smalls, kept, tensor_index):
    weight_query, weight_key, weight_value, weight_out, weight_gate, weight_up, weight_down = (
        weights
    )
    weight_router, gain_attn, gain_ffn = smalls
    (
        scale_attn,
        full_attn,
        query_grouped,
        key_rows,
        value_rows,
        visible,
        log_total,
        mixed,
        hidden,
        scale_ffn,
        normed_ffn,
        full_ffn,
        picked,
        gate_values,
        slot_of,
        source,
        gate_pre,
        up_pre,
        activated,
        cosine_table,
        sine_table,
    ) = kept
    heads_query = weight_query.shape[1] // HD
    heads_kv = weight_key.shape[1] // HD
    shard_rows = entering.shape[0]
    group_rows = full_ffn.shape[0]
    capacity = slot_count(group_rows)
    full_grad = spread(grad_result.astype(jnp.bfloat16))
    padded_grad = jnp.concatenate(
        [full_grad, jnp.zeros((1, full_grad.shape[1]), jnp.bfloat16)], axis=0
    )
    grad_slots = padded_grad[source].astype(jnp.float32)
    gate_slots = jnp.zeros((E * capacity,), jnp.float32).at[slot_of].set(gate_values.reshape(-1))
    expert_out = jnp.einsum(
        "ecf,efd->ecd", activated, weight_down, preferred_element_type=jnp.float32
    ).reshape(E * capacity, -1)
    gate_grad_part = jnp.sum(grad_slots * expert_out, axis=-1)[slot_of].reshape(group_rows, TOP)
    grad_expert = (gate_slots[:, None] * grad_slots).astype(jnp.bfloat16).reshape(E, capacity, -1)
    grad_act = jnp.einsum(
        "ecd,efd->ecf", grad_expert, weight_down, preferred_element_type=jnp.float32
    )
    sigma = jax.nn.sigmoid(gate_pre)
    grad_gate_pre = (grad_act * up_pre * sigma * (1.0 + gate_pre * (1.0 - sigma))).astype(
        jnp.bfloat16
    )
    grad_up_pre = (grad_act * gate_pre * sigma).astype(jnp.bfloat16)
    grad_in = jnp.einsum(
        "ecf,edf->ecd", grad_gate_pre, weight_gate, preferred_element_type=jnp.float32
    )
    grad_in = grad_in + jnp.einsum(
        "ecf,edf->ecd", grad_up_pre, weight_up, preferred_element_type=jnp.float32
    )
    grad_tokens = jnp.sum(
        grad_in.reshape(E * capacity, -1)[slot_of].reshape(group_rows, TOP, -1), axis=1
    )
    grad_normed_ffn, grad_gate_values = (
        lax.psum_scatter(
            grad_tokens.astype(jnp.bfloat16), "tensor", scatter_dimension=0, tiled=True
        ).astype(jnp.float32),
        lax.psum_scatter(
            gate_grad_part.astype(jnp.bfloat16), "tensor", scatter_dimension=0, tiled=True
        ).astype(jnp.float32),
    )
    row_start = tensor_index * shard_rows
    gates_own = lax.dynamic_slice_in_dim(gate_values, row_start, shard_rows, 0)
    picked_own = lax.dynamic_slice_in_dim(picked, row_start, shard_rows, 0)
    grad_chosen = gates_own * (
        grad_gate_values - jnp.sum(gates_own * grad_gate_values, axis=-1, keepdims=True)
    )
    grad_logits = jnp.sum(jnp.where(picked_own, grad_chosen[:, :, None], 0.0), axis=1).astype(
        jnp.bfloat16
    )
    grad_router = jnp.einsum(
        "td,te->de", normed_ffn, grad_logits, preferred_element_type=jnp.float32
    )
    grad_normed_ffn = grad_normed_ffn + jnp.dot(
        grad_logits, weight_router.T, preferred_element_type=jnp.float32
    )
    grad_hidden_part, grad_gain_ffn = norm_back(hidden, scale_ffn, gain_ffn, grad_normed_ffn)
    grad_hidden = grad_result + grad_hidden_part
    full_grad_attn = spread(grad_hidden.astype(jnp.bfloat16))
    grad_weight_out = jnp.einsum(
        "tc,td->cd", mixed, full_grad_attn, preferred_element_type=jnp.float32
    )
    grad_mixed = jnp.dot(full_grad_attn, weight_out.T, preferred_element_type=jnp.float32).astype(
        jnp.bfloat16
    )
    grad_mixed = grad_mixed.reshape(group_rows, heads_kv, heads_query // heads_kv, HD)
    scores = attention_scores(query_grouped, key_rows, visible)
    soft_full = jnp.exp(scores - log_total)
    soft_low = soft_full.astype(jnp.bfloat16)
    grad_soft = jnp.einsum(
        "tkgd,skd->kgts", grad_mixed, value_rows, preferred_element_type=jnp.float32
    )
    grad_values = jnp.einsum(
        "kgts,tkgd->skd", soft_low, grad_mixed, preferred_element_type=jnp.float32
    )
    grad_values = grad_values.astype(jnp.bfloat16).reshape(group_rows, heads_kv * HD)
    grad_scores = (
        soft_full * (grad_soft - jnp.sum(soft_full * grad_soft, axis=-1, keepdims=True))
    ).astype(jnp.bfloat16)
    grad_query = jnp.einsum(
        "kgts,skd->tkgd", grad_scores, key_rows, preferred_element_type=jnp.float32
    ) * HD ** (-0.5)
    grad_keys = jnp.einsum(
        "kgts,tkgd->skd", grad_scores, query_grouped, preferred_element_type=jnp.float32
    ) * HD ** (-0.5)
    grad_query = rotate(grad_query.reshape(group_rows, heads_query, HD), cosine_table, -sine_table)
    grad_query = grad_query.reshape(group_rows, heads_query * HD).astype(jnp.bfloat16)
    grad_keys = (
        rotate(grad_keys, cosine_table, -sine_table)
        .reshape(group_rows, heads_kv * HD)
        .astype(jnp.bfloat16)
    )
    grad_weight_query = jnp.einsum(
        "tc,te->ce", full_attn, grad_query, preferred_element_type=jnp.float32
    )
    grad_weight_key = jnp.einsum(
        "tc,te->ce", full_attn, grad_keys, preferred_element_type=jnp.float32
    )
    grad_weight_value = jnp.einsum(
        "tc,te->ce", full_attn, grad_values, preferred_element_type=jnp.float32
    )
    grad_full_attn = jnp.dot(grad_query, weight_query.T, preferred_element_type=jnp.float32)
    grad_full_attn = grad_full_attn + jnp.dot(
        grad_keys, weight_key.T, preferred_element_type=jnp.float32
    )
    grad_full_attn = grad_full_attn + jnp.dot(
        grad_values, weight_value.T, preferred_element_type=jnp.float32
    )
    grad_normed_attn = collect(grad_full_attn)
    grad_entering_part, grad_gain_attn = norm_back(
        entering, scale_attn, gain_attn, grad_normed_attn
    )
    grad_entering = grad_hidden + grad_entering_part
    grads = (
        grad_gain_attn,
        grad_weight_query,
        grad_weight_key,
        grad_weight_value,
        grad_weight_out,
        grad_router,
        grad_gain_ffn,
    )
    terms = (
        expert_rows(full_ffn, source, capacity),
        grad_gate_pre,
        grad_up_pre,
        activated,
        grad_expert,
    )
    return (grad_entering, grads, terms)


def per_device(
    inputs,
    cotangent,
    doc_lengths,
    routes,
    norm_attn,
    w_query,
    w_key,
    w_value,
    w_out,
    w_router,
    norm_ffn,
    w_gate,
    w_up,
    w_down,
):
    first_section = lax.axis_index("pipe") == 0
    section_index = lax.axis_index("pipe")
    tensor_index = lax.axis_index("tensor")
    micro = inputs.shape[0]
    group_rows = inputs.shape[1] * lax.axis_size("tensor")
    pieces = (w_query[0], w_key[0], w_value[0], w_out[0], w_gate[0], w_up[0], w_down[0])
    weights = (
        lax.all_gather(pieces[0], "dp", axis=0, tiled=True),
        lax.all_gather(pieces[1], "dp", axis=0, tiled=True),
        lax.all_gather(pieces[2], "dp", axis=0, tiled=True),
        lax.all_gather(pieces[3], "dp", axis=1, tiled=True),
        lax.all_gather(pieces[4], "dp", axis=1, tiled=True),
        lax.all_gather(pieces[5], "dp", axis=1, tiled=True),
        lax.all_gather(pieces[6], "dp", axis=2, tiled=True),
    )
    router_full, gain_attn, gain_ffn = (
        lax.all_gather(w_router[0], ("dp", "tensor"), axis=0, tiled=True),
        lax.all_gather(norm_attn[0], ("dp", "tensor"), axis=0, tiled=True),
        lax.all_gather(norm_ffn[0], ("dp", "tensor"), axis=0, tiled=True),
    )
    smalls = (router_full, gain_attn.astype(jnp.float32), gain_ffn.astype(jnp.float32))
    lengths_local = doc_lengths[:, 0]
    received = jnp.zeros(inputs.shape[1:], jnp.bfloat16)
    outputs = []
    saves = []
    for tick_no in range(micro + 1):
        micro_no = jnp.clip(tick_no - section_index, 0, micro - 1)
        own_rows = lax.dynamic_index_in_dim(inputs, micro_no, 0, keepdims=False)
        entering = jnp.where(first_section, own_rows, received).astype(jnp.float32)
        chosen_ids = lax.dynamic_index_in_dim(routes[0], micro_no, 0, keepdims=False)
        lengths = lax.dynamic_index_in_dim(lengths_local, micro_no, 0, keepdims=False)
        segment, position = doc_layout(lengths, group_rows)
        result, kept = layer_forward(entering, weights, smalls, chosen_ids, segment, position)
        sent = result.astype(jnp.bfloat16)
        outputs.append(sent)
        saves.append((entering, kept))
        if tick_no < micro:
            received = shifted(sent, "pipe", 1)
    weights = (
        lax.all_gather(pieces[0], "dp", axis=0, tiled=True),
        lax.all_gather(pieces[1], "dp", axis=0, tiled=True),
        lax.all_gather(pieces[2], "dp", axis=0, tiled=True),
        lax.all_gather(pieces[3], "dp", axis=1, tiled=True),
        lax.all_gather(pieces[4], "dp", axis=1, tiled=True),
        lax.all_gather(pieces[5], "dp", axis=1, tiled=True),
        lax.all_gather(pieces[6], "dp", axis=2, tiled=True),
    )
    arriving = jnp.zeros(inputs.shape[1:], jnp.bfloat16)
    grads_in = []
    totals = None
    expert_terms = []
    for tick_no in range(micro + 1):
        target = tick_no - 1 + section_index
        micro_no = jnp.clip(target, 0, micro - 1)
        is_live = (target >= 0) & (target < micro)
        own_cot = lax.dynamic_index_in_dim(cotangent, micro_no, 0, keepdims=False)
        own_cot = jnp.where(is_live, own_cot, jnp.zeros_like(own_cot))
        incoming = jnp.where(first_section, arriving, own_cot).astype(jnp.float32)
        lower_tick = max(tick_no - 1, 0)
        upper_tick = min(tick_no + 1, micro)
        entering, kept = jax.tree.map(
            lambda left_val, right_val: jnp.where(first_section, left_val, right_val),
            saves[lower_tick],
            saves[upper_tick],
        )
        grad_entering, grads, terms = layer_backward(
            entering, incoming, weights, smalls, kept, tensor_index
        )
        grads_in.append(grad_entering)
        totals = grads if totals is None else jax.tree.map(jnp.add, totals, grads)
        if tick_no < micro:
            arriving = shifted(grad_entering.astype(jnp.bfloat16), "pipe", -1)
        expert_terms.append(terms)
    (
        grad_gain_attn,
        grad_weight_query,
        grad_weight_key,
        grad_weight_value,
        grad_weight_out,
        grad_router,
        grad_gain_ffn,
    ) = totals
    joined = tuple(
        (jnp.concatenate([terms[member] for terms in expert_terms], axis=1) for member in range(5))
    )
    grad_weight_gate, grad_weight_up, grad_weight_down = expert_grads_of(joined)
    summed = (
        lax.psum_scatter(
            grad_weight_query.astype(jnp.bfloat16), "dp", scatter_dimension=0, tiled=True
        ).astype(jnp.float32),
        lax.psum_scatter(
            grad_weight_key.astype(jnp.bfloat16), "dp", scatter_dimension=0, tiled=True
        ).astype(jnp.float32),
        lax.psum_scatter(
            grad_weight_value.astype(jnp.bfloat16), "dp", scatter_dimension=0, tiled=True
        ).astype(jnp.float32),
        lax.psum_scatter(
            grad_weight_out.astype(jnp.bfloat16), "dp", scatter_dimension=1, tiled=True
        ).astype(jnp.float32),
        lax.psum_scatter(
            grad_weight_gate.astype(jnp.bfloat16), "dp", scatter_dimension=1, tiled=True
        ).astype(jnp.float32),
        lax.psum_scatter(
            grad_weight_up.astype(jnp.bfloat16), "dp", scatter_dimension=1, tiled=True
        ).astype(jnp.float32),
        lax.psum_scatter(
            grad_weight_down.astype(jnp.bfloat16), "dp", scatter_dimension=2, tiled=True
        ).astype(jnp.float32),
    )
    small_sums = (
        lax.psum_scatter(grad_router, ("dp", "tensor"), scatter_dimension=0, tiled=True),
        lax.psum_scatter(grad_gain_attn, ("dp", "tensor"), scatter_dimension=0, tiled=True),
        lax.psum_scatter(grad_gain_ffn, ("dp", "tensor"), scatter_dimension=0, tiled=True),
    )
    section_rows = jnp.stack(
        [
            jnp.where(first_section, outputs[micro_no], outputs[micro_no + 1])
            for micro_no in range(micro)
        ]
    )
    grad_rows = jnp.stack(
        [
            jnp.where(first_section, grads_in[micro_no + 1], grads_in[micro_no])
            for micro_no in range(micro)
        ]
    )
    return (
        section_rows[None],
        grad_rows[None],
        small_sums[1][None],
        summed[0][None],
        summed[1][None],
        summed[2][None],
        summed[3][None],
        small_sums[0][None],
        small_sums[2][None],
        summed[4][None],
        summed[5][None],
        summed[6][None],
    )


def solution(mesh):
    in_specs = (
        P(None, ("dp", "tensor"), None),
        P(None, ("dp", "tensor"), None),
        P(None, "dp", None),
        P("pipe", None, "dp", None),
        P("pipe", ("dp", "tensor")),
        P("pipe", "dp", "tensor"),
        P("pipe", "dp", "tensor"),
        P("pipe", "dp", "tensor"),
        P("pipe", "tensor", "dp"),
        P("pipe", ("dp", "tensor"), None),
        P("pipe", ("dp", "tensor")),
        P("pipe", None, "dp", "tensor"),
        P("pipe", None, "dp", "tensor"),
        P("pipe", None, "tensor", "dp"),
    )
    out_specs = (
        P("pipe", None, ("dp", "tensor"), None),
        P("pipe", None, ("dp", "tensor"), None),
        P("pipe", ("dp", "tensor")),
        P("pipe", "dp", "tensor"),
        P("pipe", "dp", "tensor"),
        P("pipe", "dp", "tensor"),
        P("pipe", "tensor", "dp"),
        P("pipe", ("dp", "tensor"), None),
        P("pipe", ("dp", "tensor")),
        P("pipe", None, "dp", "tensor"),
        P("pipe", None, "dp", "tensor"),
        P("pipe", None, "tensor", "dp"),
    )
    return jax.shard_map(
        per_device, mesh=mesh, in_specs=in_specs, out_specs=out_specs, check_vma=False
    )
```

profile of v0, /device:TPU:0, one launch (start us, length us, event | category | flops | bytes accessed | tf_op | source)
XLA Modules:
  0.0 1918.2 jit_solution(6937039801166051954)
XLA Ops:
  11.8 144.7 %all-reduce.14 = (bf16[1024]{0:T(1024)(128)(2,1)S(1)}, bf16[1024]{0:T(1024)(128)(2,1)S(1)}) all-reduce(bf16[1024]{0:T(1024)(128)(2,1)S(1)} %dynamic-update-slice, bf16[1024]{0:T(1024)(128)(2,1)S(1)} %dynamic-update-slice.1), channel_id=2, replica_groups=mesh['pipe'=2,'dp'=16,'tensor'=4] {'dp','tensor'}, use_global_device_ids=true, to_apply=%add.9 | all-reduce | flops 2048 | bytes 8192
  171.4 16.9 all-gather.1
  188.3 19.5 %all-gather.3 = bf16[1,1024,256]{2,1,0:T(8,128)(2,1)S(1)} all-gather(bf16[1,64,256]{2,1,0:T(8,128)(2,1)} %param.19), channel_id=5, replica_groups=mesh['pipe'=2,'dp'=16,'tensor'=4] {'dp'}, dimensions={1}, use_global_device_ids=true | all-gather | bytes 557056 | tf_op jit(solution)/shard_map/all_gather | solution.py:389
  210.7 17.2 all-gather.2
  231.1 19.1 all-gather.4
  296.7 138.4 %all-gather.6 = bf16[1,1024,16]{2,1,0:T(8,128)(2,1)S(1)} all-gather(bf16[1,16,16]{2,1,0:T(8,128)(2,1)S(1)} %copy-done.243), channel_id=8, replica_groups=mesh['pipe'=2,'dp'=16,'tensor'=4] {'dp','tensor'}, dimensions={1}, use_global_device_ids=true | all-gather | bytes 33280 | tf_op jit(solution)/shard_map/all_gather | solution.py:398
  486.6 15.7 gather_fusion.1
  509.2 19.6 %reduce-scatter.32.cloned.1.call-done = bf16[64,1024]{1,0:T(8,128)(2,1)} async-done(((bf16[256,1024]{1,0:T(8,128)(2,1)}), bf16[64,1024]{1,0:T(8,128)(2,1)}) %reduce-scatter.32.cloned.1.call-update) | async-done | bytes 131088 | tf_op jit(solution)/shard_map/reduce_scatter | solution.py:94
  667.4 15.7 gather_fusion.7
  697.5 15.8 gather_fusion.3
  749.7 16.3 reduce-scatter.44.cloned.1.call-done
  797.0 14.7 all_gather.91
  904.9 15.7 gather_fusion.10
  928.9 17.7 reduce-scatter.46.cloned.1.call-done
  975.1 16.7 reduce-scatter.48.cloned.1.call-done
  1069.7 15.8 gather_fusion.13
  1099.9 15.8 gather_fusion.5
  1227.6 44.9 %reduce-scatter.58.cloned.1.call-done = bf16[64,128]{1,0:T(8,128)(2,1)} async-done(((bf16[1024,128]{1,0:T(8,128)(2,1)}), bf16[64,128]{1,0:T(8,128)(2,1)}) %reduce-scatter.58.cloned.1.call-update) | async-done | bytes 16400 | tf_op jit(solution)/shard_map/reduce_scatter | solution.py:475
  1273.9 21.4 %reduce-scatter.52.cloned.1.call-done = bf16[64,1024]{1,0:T(8,128)(2,1)} async-done(((bf16[256,1024]{1,0:T(8,128)(2,1)}), bf16[64,1024]{1,0:T(8,128)(2,1)}) %reduce-scatter.52.cloned.1.call-update) | async-done | bytes 131088 | tf_op jit(solution)/shard_map/reduce_scatter | solution.py:94
  1296.5 142.4 %all-reduce.13 = (f32[1024]{0:T(1024)S(1)}, f32[1024]{0:T(1024)S(1)}) all-reduce(f32[1024]{0:T(1024)S(1)} %add_add_fusion.1, f32[1024]{0:T(1024)S(1)} %add_add_fusion), channel_id=28, replica_groups=mesh['pipe'=2,'dp'=16,'tensor'=4] {'dp','tensor'}, use_global_device_ids=true, to_apply=%region_87.88.clone | all-reduce | flops 2048 | bytes 16384
  1444.8 43.4 %reduce-scatter.64.cloned.1.call-done = bf16[16,64,128]{2,1,0:T(8,128)(2,1)} async-done(((bf16[16,1024,128]{2,1,0:T(8,128)(2,1)}), bf16[16,64,128]{2,1,0:T(8,128)(2,1)}) %reduce-scatter.64.cloned.1.call-update) | async-done | bytes 262160 | tf_op jit(solution)/shard_map/reduce_scatter | solution.py:481
  1490.0 66.2 %reduce-scatter.66.cloned.1.call-done = bf16[16,64,128]{2,1,0:T(8,128)(2,1)} async-done(((bf16[16,1024,128]{2,1,0:T(8,128)(2,1)}), bf16[16,64,128]{2,1,0:T(8,128)(2,1)}) %reduce-scatter.66.cloned.1.call-update) | async-done | bytes 262160 | tf_op jit(solution)/shard_map/reduce_scatter | solution.py:484
  1558.0 66.3 %reduce-scatter.68.cloned.1.call-done = bf16[16,128,64]{1,2,0:T(8,128)(2,1)} async-done(((bf16[16,128,1024]{1,2,0:T(8,128)(2,1)}), bf16[16,128,64]{1,2,0:T(8,128)(2,1)}) %reduce-scatter.68.cloned.1.call-update) | async-done | bytes 262160 | tf_op jit(solution)/shard_map/reduce_scatter | solution.py:487
  1626.0 284.7 %reduce-scatter.62.cloned.1.call-done = f32[16,16]{1,0:T(8,128)} async-done(((f32[1024,16]{1,0:T(8,128)}), f32[16,16]{1,0:T(8,128)}) %reduce-scatter.62.cloned.1.call-update) | async-done | bytes 1040 | tf_op jit(solution)/shard_map/reduce_scatter | solution.py:492
  (946 shorter events, 692.0 us)
Async XLA Ops:
  8.0 427.8 %reduce-scatter.30.cloned.1.call-start = ((), (), s32[]{:S(2)}) async-start(), calls=%async_computation.23 | async-start | bytes 655360 | tf_op jit(solution)/shard_map/reduce_scatter | solution.py:94
  251.7 209.6 %all-gather.19.cloned.1.call-start = ((), (), s32[]{:S(2)}) async-start(), calls=%async_computation.45 | async-start | bytes 4456448 | tf_op jit(solution)/shard_map/all_gather | solution.py:395
  252.6 215.3 %all-gather.15.cloned.1.call-start = ((), (), s32[]{:S(2)}) async-start(), calls=%async_computation.43 | async-start | bytes 4456448 | tf_op jit(solution)/shard_map/all_gather | solution.py:393
  253.2 221.1 %all-gather.17.cloned.1.call-start = ((), (), s32[]{:S(2)}) async-start(), calls=%async_computation.44 | async-start | bytes 4456448 | tf_op jit(solution)/shard_map/all_gather | solution.py:394
  253.8 275.0 %reduce-scatter.32.cloned.1.call-start = ((), (), s32[]{:S(2)}) async-start(), calls=%async_computation.24 | async-start | bytes 655360 | tf_op jit(solution)/shard_map/reduce_scatter | solution.py:94
  509.1 76.8 %reduce-scatter.34.cloned.1.call-start = ((), (), s32[]{:S(2)}) async-start(), calls=%async_computation.25 | async-start | bytes 655360 | tf_op jit(solution)/shard_map/reduce_scatter | solution.py:94
  567.0 153.2 %reduce-scatter.70.cloned.1.call-start = ((), (), s32[]{:S(2)}) async-start(), calls=%async_computation.46 | async-start | bytes 81920
  638.6 82.8 %reduce-scatter.42.cloned.1.call-start = ((), (), s32[]{:S(2)}) async-start(), calls=%async_computation.29 | async-start | bytes 655360 | tf_op jit(solution)/shard_map/reduce_scatter | solution.py:268
  742.9 77.8 %reduce-scatter.38.cloned.1.call-start = ((), (), s32[]{:S(2)}) async-start(), calls=%async_computation.27 | async-start | bytes 655360 | tf_op jit(solution)/shard_map/reduce_scatter | solution.py:94
  787.9 139.8 %reduce-scatter.72.cloned.1.call-start = ((), (), s32[]{:S(2)}) async-start(), calls=%async_computation.47 | async-start | bytes 81920
  875.8 70.8 %reduce-scatter.46.cloned.1.call-start = ((), (), s32[]{:S(2)}) async-start(), calls=%async_computation.31 | async-start | bytes 655360 | tf_op jit(solution)/shard_map/reduce_scatter | solution.py:268
  927.0 64.8 %reduce-scatter.48.cloned.1.call-start = ((), (), s32[]{:S(2)}) async-start(), calls=%async_computation.32 | async-start | bytes 655360 | tf_op jit(solution)/shard_map/reduce_scatter | solution.py:94
  969.7 155.6 %reduce-scatter.74.cloned.1.call-start = ((), (), s32[]{:S(2)}) async-start(), calls=%async_computation.48 | async-start | bytes 81920
  1050.2 77.0 %reduce-scatter.50.cloned.1.call-start = ((), (), s32[]{:S(2)}) async-start(), calls=%async_computation.33 | async-start | bytes 655360 | tf_op jit(solution)/shard_map/reduce_scatter | solution.py:268
  1091.7 131.6 %reduce-scatter.40.cloned.1.call-start = ((), (), s32[]{:S(2)}) async-start(), calls=%async_computation.28 | async-start | bytes 655360 | tf_op jit(solution)/shard_map/reduce_scatter | solution.py:94
  1122.6 103.7 %reduce-scatter.56.cloned.1.call-start = ((), (), s32[]{:S(2)}) async-start(), calls=%async_computation.36 | async-start | bytes 278528 | tf_op jit(solution)/shard_map/reduce_scatter | solution.py:472
  1148.7 123.8 %reduce-scatter.58.cloned.1.call-start = ((), (), s32[]{:S(2)}) async-start(), calls=%async_computation.37 | async-start | bytes 278528 | tf_op jit(solution)/shard_map/reduce_scatter | solution.py:475
  1151.2 144.1 %reduce-scatter.52.cloned.1.call-start = ((), (), s32[]{:S(2)}) async-start(), calls=%async_computation.34 | async-start | bytes 655360 | tf_op jit(solution)/shard_map/reduce_scatter | solution.py:94
  1154.1 287.9 %reduce-scatter.54.cloned.1.call-start = ((), (), s32[]{:S(2)}) async-start(), calls=%async_computation.35 | async-start | bytes 557056 | tf_op jit(solution)/shard_map/reduce_scatter | solution.py:469
  1159.2 284.2 %reduce-scatter.60.cloned.1.call-start = ((), (), s32[]{:S(2)}) async-start(), calls=%async_computation.38 | async-start | bytes 557056 | tf_op jit(solution)/shard_map/reduce_scatter | solution.py:478
  1190.6 297.6 %reduce-scatter.64.cloned.1.call-start = ((), (), s32[]{:S(2)}) async-start(), calls=%async_computation.40 | async-start | bytes 4456448 | tf_op jit(solution)/shard_map/reduce_scatter | solution.py:481
  1201.2 354.9 %reduce-scatter.66.cloned.1.call-start = ((), (), s32[]{:S(2)}) async-start(), calls=%async_computation.41 | async-start | bytes 4456448 | tf_op jit(solution)/shard_map/reduce_scatter | solution.py:484
  1211.3 412.9 %reduce-scatter.68.cloned.1.call-start = ((), (), s32[]{:S(2)}) async-start(), calls=%async_computation.42 | async-start | bytes 4456448 | tf_op jit(solution)/shard_map/reduce_scatter | solution.py:487
  1221.9 688.8 %reduce-scatter.62.cloned.1.call-start = ((), (), s32[]{:S(2)}) async-start(), calls=%async_computation.39 | async-start | bytes 532480 | tf_op jit(solution)/shard_map/reduce_scatter | solution.py:492
  (270 other events, 8860.0 us)
Sparse Core Ops, SparseCore 0:
  251.8 19.0 reduce-scatter.29
  509.2 19.5 reduce-scatter.31
  567.2 18.6 reduce-scatter.33
  638.7 19.9 reduce-scatter.69
  689.7 21.1 reduce-scatter.41
  720.2 21.5 reduce-scatter.35
  744.9 21.0 reduce-scatter.43
  788.0 20.9 reduce-scatter.37
  875.9 18.1 reduce-scatter.71
  927.2 19.3 reduce-scatter.45
  969.9 21.9 reduce-scatter.47
  1050.3 21.6 reduce-scatter.73
  1091.9 22.8 reduce-scatter.49
  1122.7 23.6 reduce-scatter.39
  1148.8 62.7 reduce-scatter.55
  1213.8 58.7 reduce-scatter.57
  1275.5 19.7 reduce-scatter.51
  1298.2 60.4 reduce-scatter.53
  1361.0 59.3 reduce-scatter.59
  1422.8 65.3 reduce-scatter.63
  1490.7 65.3 reduce-scatter.65
  1558.7 65.4 reduce-scatter.67
  1627.3 283.3 reduce-scatter.61
Sparse Core Ops, SparseCore 1:
  254.4 35.4 all-gather.18
  291.4 37.7 all-gather.14
  330.7 37.6 all-gather.16
where the time goes:
time: 1930 us; the launch traced here: 1920 us
  blocking collectives  657 us (34%)
  waiting for transfers between devices  613 us (32%)
  local copies, waits for them, and re-layouts  304 us (16%)
  matrix products  186 us (10%)
  other arithmetic  121 us (6%)
  between operations  21.4 us (1%)
    unnamed x2, blocking collectives  287 us
    reduce_scatter x1, waiting for transfers between devices, per_device(): lax.psum_scatter(grad_router, ('dp', 'tensor'), scatter_dimension=0, tile...  285 us
    all_gather x12, blocking collectives, spread(): return lax.all_gather(shard_rows, 'tensor', axis=0, tiled=True)  159 us
    all_gather x1, blocking collectives, per_device(): lax.all_gather(w_router[0], ('dp', 'tensor'), axis=0, tiled=True)  138 us
    reduce_scatter x9, waiting for transfers between devices, collect(): lax.psum_scatter(partial_rows.astype(jnp.bfloat16), 'tensor', scatter_dim...  82.2 us
    reduce_scatter x1, waiting for transfers between devices, per_device(): lax.psum_scatter(grad_weight_down.astype(jnp.bfloat16), 'dp', scatter_dim...  66.3 us
    reduce_scatter x1, waiting for transfers between devices, per_device(): lax.psum_scatter(grad_weight_up.astype(jnp.bfloat16), 'dp', scatter_dimen...  66.2 us
    gather x6, local copies, waits for them, and re-layouts, expert_rows(): return padded[source].reshape(E, capacity, full_rows.shape[1])  53.5 us
  transfers between devices with their start and end apart: 30, of which 12 were waited for; matrix products, arithmetic and copies ran while one was open for 22% of the time, Pallas kernels for 0%

commit v1 on v0

v1 whole, which is shorter than its diff:
```python
import math

import jax
import jax.numpy as jnp
from jax import lax
from jax.experimental import pallas as pl
from jax.experimental.pallas import tpu as pltpu
from jax.sharding import PartitionSpec as P

HD = 64
E = 16
TOP = 8
EPSILON = 1e-06
MASKED = -1000000000.0
BF = jnp.bfloat16
F32 = jnp.float32
VMEM_LIMIT = 56 * 1024 * 1024
PER = 2
LANES = 128


def params():
    return pltpu.CompilerParams(
        vmem_limit_bytes=VMEM_LIMIT, dimension_semantics=("arbitrary",)
    )


def dot(left, right):
    return jnp.dot(left, right, preferred_element_type=F32)


def dot_nt(left, right):
    return lax.dot_general(
        left, right, (((1,), (1,)), ((), ())), preferred_element_type=F32
    )


def dot_tn(left, right):
    return lax.dot_general(
        left, right, (((0,), (0,)), ((), ())), preferred_element_type=F32
    )


def column(rows, index):
    lanes = lax.broadcasted_iota(jnp.int32, rows.shape, 1)
    return jnp.sum(jnp.where(lanes == index, rows, 0.0), axis=1, keepdims=True)


def whole(shape):
    return pl.BlockSpec(shape, lambda i, s: (0,) * len(shape))


def rms_scale(values):
    return lax.rsqrt(jnp.mean(values * values, axis=-1, keepdims=True) + EPSILON)


def norm_back(values, scale_rows, gain, grad_normed):
    weighted = grad_normed * gain
    grad_values = scale_rows * weighted - values * scale_rows**3 * jnp.mean(
        weighted * values, axis=-1, keepdims=True
    )
    grad_gain = jnp.sum(grad_normed * values * scale_rows, axis=0, keepdims=True)
    return grad_values, grad_gain


def swap_halves(values):
    width = values.shape[1]
    lanes = lax.broadcasted_iota(jnp.int32, values.shape, 1)
    ahead = pltpu.roll(values, width - HD // 2, 1)
    behind = pltpu.roll(values, HD // 2, 1)
    return jnp.where(lanes % HD < HD // 2, ahead, behind)


def assemble(me, pieces, peers, target, extra=None):
    rows = pieces[0].shape[0]
    for shift in range(peers):
        owner = lax.rem(me + peers - shift, peers)
        place = pl.ds(pl.multiple_of(owner * rows, rows), rows)
        block = pieces[shift][...]
        if extra is not None:
            block = block + extra[place, :]
        target[place, :] = block


def own_rows(me, rows):
    return pl.ds(pl.multiple_of(me * rows, rows), rows)


def attention_forward_kernel(n_pieces, has_full, *refs):
    (sref, *refs) = refs
    pieces, refs = refs[:n_pieces], refs[n_pieces:]
    full_ref = None
    if has_full:
        full_ref, refs = refs[0], refs[1:]
    (
        gains_ref,
        cos_ref,
        sin_ref,
        bias_ref,
        picked_ref,
        w_ref,
        router_ref,
        a_ref,
        xown_ref,
        qkv_ref,
        o_ref,
        lse_ref,
        hown_ref,
        b_ref,
        gates_ref,
        hidden,
        rows_in,
    ) = refs
    step = pl.program_id(0)
    me = sref[0]
    group, width = b_ref.shape
    shard = xown_ref.shape[0]

    @pl.when(step == 0)
    def _():
        if n_pieces:
            assemble(me, pieces, n_pieces, rows_in, full_ref)
        else:
            rows_in[...] = full_ref[...]
        entering = rows_in[...].astype(F32)
        a_ref[...] = (entering * rms_scale(entering) * gains_ref[0:1, :]).astype(BF)
        xown_ref[...] = rows_in[own_rows(me, shard), :]
        hidden[...] = entering

    weights = w_ref[:, 0].reshape(width, -1)
    qkv = dot(a_ref[...], weights[:, :512])
    qk = qkv[:, :384]
    cos = jnp.concatenate([cos_ref[0]] * 3, axis=1)
    sin = jnp.concatenate([sin_ref[0]] * 3, axis=1)
    turned = qk * cos + swap_halves(qk) * sin
    q = (turned[:, :256] * HD**-0.5).astype(BF)
    k = turned[:, 256:].astype(BF)
    v = qkv[:, 384:].astype(BF)
    qkv_ref[0, :, :256] = q
    qkv_ref[0, :, 256:384] = k
    qkv_ref[0, :, 384:] = v
    bias = bias_ref[0]
    lanes = lax.broadcasted_iota(jnp.int32, (group, LANES), 1)
    lse_all = jnp.zeros((group, LANES), F32)
    outs = []
    for head in range(4):
        kv = head // 2
        scores = dot_nt(q[:, head * HD : (head + 1) * HD], k[:, kv * HD : (kv + 1) * HD])
        scores = scores + bias
        peak = jnp.max(scores, axis=1, keepdims=True)
        soft = jnp.exp(scores - peak)
        total = jnp.sum(soft, axis=1, keepdims=True)
        lse_all = jnp.where(lanes == head, peak + jnp.log(total), lse_all)
        soft = (soft * (1.0 / total)).astype(BF)
        outs.append(dot(soft, v[:, kv * HD : (kv + 1) * HD]))
    mixed = jnp.concatenate(outs, axis=1).astype(BF)
    o_ref[0] = mixed
    lse_ref[0] = lse_all
    hidden[...] += dot_nt(mixed, weights[:, 512:])

    @pl.when(step == pl.num_programs(0) - 1)
    def _():
        rows = hidden[...]
        normed = (rows * rms_scale(rows) * gains_ref[1:2, :]).astype(BF)
        b_ref[...] = normed
        hown_ref[...] = hidden[own_rows(me, shard), :]
        logits = dot(normed, router_ref[...])
        picked = picked_ref[0]
        peak = jnp.max(jnp.where(picked > 0, logits, -1e30), axis=1, keepdims=True)
        powers = jnp.where(picked > 0, jnp.exp(jnp.minimum(logits - peak, 0.0)), 0.0)
        gates_ref[...] = powers / jnp.sum(powers, axis=1, keepdims=True)


def attention_forward(scalars, pieces, full, gains, tables, picked, w_attn, router):
    dp, peers, dr, cols = w_attn.shape
    width = dp * dr
    group = tables[0].shape[1]
    shard = group // peers
    cos, sin, bias = tables
    pick = lambda i, s: (s[1], 0, 0)
    operands = [*pieces] + ([full] if full is not None else [])
    in_specs = [whole(x.shape) for x in operands] + [
        whole(gains.shape),
        pl.BlockSpec((1,) + cos.shape[1:], pick),
        pl.BlockSpec((1,) + sin.shape[1:], pick),
        pl.BlockSpec((1,) + bias.shape[1:], pick),
        pl.BlockSpec((1,) + picked.shape[1:], pick),
        pl.BlockSpec((dp, 1, dr, cols), lambda i, s: (0, i, 0, 0)),
        whole(router.shape),
    ]
    per_step = lambda i, s: (i, 0, 0)
    out_shape = [
        jax.ShapeDtypeStruct((group, width), BF),
        jax.ShapeDtypeStruct((shard, width), BF),
        jax.ShapeDtypeStruct((peers, group, 512), BF),
        jax.ShapeDtypeStruct((peers, group, 256), BF),
        jax.ShapeDtypeStruct((peers, group, LANES), F32),
        jax.ShapeDtypeStruct((shard, width), F32),
        jax.ShapeDtypeStruct((group, width), BF),
        jax.ShapeDtypeStruct((group, E), F32),
    ]
    out_specs = [
        whole((group, width)),
        whole((shard, width)),
        pl.BlockSpec((1, group, 512), per_step),
        pl.BlockSpec((1, group, 256), per_step),
        pl.BlockSpec((1, group, LANES), per_step),
        whole((shard, width)),
        whole((group, width)),
        whole((group, E)),
    ]
    return pl.pallas_call(
        lambda *refs: attention_forward_kernel(len(pieces), full is not None, *refs),
        grid_spec=pltpu.PrefetchScalarGridSpec(
            num_scalar_prefetch=1,
            grid=(peers,),
            in_specs=in_specs,
            out_specs=out_specs,
            scratch_shapes=[pltpu.VMEM((group, width), F32), pltpu.VMEM((group, width), BF)],
        ),
        out_shape=out_shape,
        compiler_params=params(),
        cost_estimate=pl.CostEstimate(
            flops=2 * group * width * cols * peers + 16 * 4 * group * group * HD,
            bytes_accessed=w_attn.size * 2 + 6 * group * width * 2,
            transcendentals=16 * group * group,
        ),
        name="attention_forward",
    )(scalars, *operands, gains, cos, sin, bias, picked, w_attn, router)


def experts_forward_kernel(peers, sref, b_ref, gate_ref, w_ref, *refs):
    pieces, (gu_ref, total) = refs[:peers], refs[peers:]
    step = pl.program_id(0)
    width = b_ref.shape[1]
    ff = w_ref.shape[-1]
    b = b_ref[...]
    gates = gate_ref[...]
    acts, downs = [], []
    for j in range(PER):
        gate_up = jnp.concatenate(
            [w_ref[:, 0, j].reshape(width, ff), w_ref[:, 1, j].reshape(width, ff)], axis=1
        )
        both = dot(b, gate_up)
        gu_ref[j] = both.astype(BF)
        gate_pre, up_pre = both[:, :ff], both[:, ff:]
        act = gate_pre * jax.nn.sigmoid(gate_pre) * up_pre
        acts.append((act * column(gates, step * PER + j)).astype(BF))
        downs.append(w_ref[:, 2, j].reshape(width, ff))
    out = dot_nt(jnp.concatenate(acts, axis=1), jnp.concatenate(downs, axis=1))

    @pl.when(step == 0)
    def _():
        total[...] = out

    @pl.when(step > 0)
    def _():
        total[...] += out

    @pl.when(step == pl.num_programs(0) - 1)
    def _():
        rows = b_ref.shape[0] // peers
        for shift in range(peers):
            place = own_rows(lax.rem(sref[0] + shift, peers), rows)
            pieces[shift][...] = total[place, :].astype(BF)


def experts_forward(scalars, b, gates, w, peers):
    group, width = b.shape
    dp, _, experts, dr, ff = w.shape
    piece = (group // peers, width)
    return pl.pallas_call(
        lambda *refs: experts_forward_kernel(peers, *refs),
        grid_spec=pltpu.PrefetchScalarGridSpec(
            num_scalar_prefetch=1,
            grid=(experts // PER,),
            in_specs=[
                whole((group, width)),
                whole((group, experts)),
                pl.BlockSpec((dp, 3, PER, dr, ff), lambda i, s: (0, 0, i, 0, 0)),
            ],
            out_specs=[whole(piece)] * peers
            + [pl.BlockSpec((PER, group, 2 * ff), lambda i, s: (i, 0, 0))],
            scratch_shapes=[pltpu.VMEM((group, width), F32)],
        ),
        out_shape=[jax.ShapeDtypeStruct(piece, BF)] * peers
        + [jax.ShapeDtypeStruct((experts, group, 2 * ff), BF)],
        compiler_params=params(),
        cost_estimate=pl.CostEstimate(
            flops=2 * group * width * ff * 3 * experts,
            bytes_accessed=w.size * 2 + experts * group * 2 * ff * 2,
            transcendentals=experts * group * ff,
        ),
        name="experts_forward",
    )(scalars, b, gates, w)


def experts_backward_kernel(peers, n_pieces, has_full, *refs):
    (sref, *refs) = refs
    given, refs = refs[:n_pieces], refs[n_pieces:]
    full_ref = None
    if has_full:
        full_ref, refs = refs[0], refs[1:]
    gate_ref, gu_ref, w_ref, *refs = refs
    pieces, refs = refs[:peers], refs[peers:]
    grad_ref, dgu_ref, ga_ref, total, total_gate = refs
    step = pl.program_id(0)
    group, width = grad_ref.shape
    ff = w_ref.shape[-1]

    @pl.when(step == 0)
    def _():
        if n_pieces:
            assemble(sref[0], given, n_pieces, grad_ref, full_ref)
        else:
            grad_ref[...] = full_ref[...]

    grad = grad_ref[...]
    gates = gate_ref[...]
    down = jnp.concatenate([w_ref[:, 2, j].reshape(width, ff) for j in range(PER)], axis=1)
    turned = dot(grad, down)
    lanes = lax.broadcasted_iota(jnp.int32, (group, LANES), 1)
    grad_gate = jnp.zeros((group, LANES), F32)
    out = None
    for j in range(PER):
        expert = step * PER + j
        back = turned[:, j * ff : (j + 1) * ff]
        both = gu_ref[j].astype(F32)
        gate_pre, up_pre = both[:, :ff], both[:, ff:]
        sigma = jax.nn.sigmoid(gate_pre)
        silu = gate_pre * sigma
        act = silu * up_pre
        gate = column(gates, expert)
        grad_gate = jnp.where(
            lanes == expert, jnp.sum(act * back, axis=1, keepdims=True), grad_gate
        )
        grad_act = gate * back
        grad_pre = (grad_act * up_pre * sigma * (1.0 + gate_pre * (1.0 - sigma))).astype(BF)
        grad_up = (grad_act * silu).astype(BF)
        grad_both = jnp.concatenate([grad_pre, grad_up], axis=1)
        dgu_ref[j] = grad_both
        ga_ref[:, j * ff : (j + 1) * ff] = (gate * act).astype(BF)
        gate_up = jnp.concatenate(
            [w_ref[:, 0, j].reshape(width, ff), w_ref[:, 1, j].reshape(width, ff)], axis=1
        )
        part = dot_nt(grad_both, gate_up)
        out = part if out is None else out + part

    @pl.when(step == 0)
    def _():
        total[...] = out
        total_gate[...] = grad_gate

    @pl.when(step > 0)
    def _():
        total[...] += out
        total_gate[...] += grad_gate

    @pl.when(step == pl.num_programs(0) - 1)
    def _():
        rows = group // peers
        for shift in range(peers):
            place = own_rows(lax.rem(sref[0] + shift, peers), rows)
            pieces[shift][:, :width] = total[place, :].astype(BF)
            pieces[shift][:, width:] = total_gate[place, :].astype(BF)


def experts_backward(scalars, given, full, gates, gu, w, peers):
    dp, _, experts, dr, ff = w.shape
    group = gates.shape[0]
    width = dp * dr
    piece = (group // peers, width + LANES)
    operands = [*given] + ([full] if full is not None else [])
    return pl.pallas_call(
        lambda *refs: experts_backward_kernel(peers, len(given), full is not None, *refs),
        grid_spec=pltpu.PrefetchScalarGridSpec(
            num_scalar_prefetch=1,
            grid=(experts // PER,),
            in_specs=[whole(x.shape) for x in operands]
            + [
                whole((group, experts)),
                pl.BlockSpec((PER, group, 2 * ff), lambda i, s: (i, 0, 0)),
                pl.BlockSpec((dp, 3, PER, dr, ff), lambda i, s: (0, 0, i, 0, 0)),
            ],
            out_specs=[whole(piece)] * peers
            + [
                whole((group, width)),
                pl.BlockSpec((PER, group, 2 * ff), lambda i, s: (i, 0, 0)),
                pl.BlockSpec((group, PER * ff), lambda i, s: (0, i)),
            ],
            scratch_shapes=[pltpu.VMEM((group, width), F32), pltpu.VMEM((group, LANES), F32)],
        ),
        out_shape=[jax.ShapeDtypeStruct(piece, BF)] * peers
        + [
            jax.ShapeDtypeStruct((group, width), BF),
            jax.ShapeDtypeStruct((experts, group, 2 * ff), BF),
            jax.ShapeDtypeStruct((group, experts * ff), BF),
        ],
        compiler_params=params(),
        cost_estimate=pl.CostEstimate(
            flops=2 * group * width * ff * 3 * experts,
            bytes_accessed=w.size * 2 + 5 * experts * group * ff * 2,
            transcendentals=experts * group * ff,
        ),
        name="experts_backward",
    )(scalars, *operands, gates, gu, w)


def middle_kernel(peers, sref, *refs):
    pieces, refs = refs[:peers], refs[peers:]
    grad_ref, hown_ref, gates_ref, b_ref, gains_ref, router_ref, dh_ref, do_ref, small_ref = refs
    rows, width = grad_ref.shape
    place = own_rows(sref[0], rows)
    joined = pieces[0][...].astype(F32)
    for shift in range(1, peers):
        joined = joined + pieces[shift][...].astype(F32)
    grad_normed = joined[:, :width]
    grad_gate = joined[:, width : width + E]
    gates = gates_ref[place, :]
    grad_logits = (
        gates * (grad_gate - jnp.sum(gates * grad_gate, axis=1, keepdims=True))
    ).astype(BF)
    normed = b_ref[place, :]
    grad_normed = grad_normed + dot_nt(grad_logits, router_ref[...])
    hidden = hown_ref[...]
    part, grad_gain = norm_back(hidden, rms_scale(hidden), gains_ref[1:2, :], grad_normed)
    grad_hidden = grad_ref[...].astype(F32) + part
    dh_ref[...] = grad_hidden
    do_ref[...] = grad_hidden.astype(BF)
    small_ref[0:E, :] = dot_tn(grad_logits, normed)
    small_ref[E : E + 1, :] = grad_gain
    small_ref[E + 1 :, :] = jnp.zeros((small_ref.shape[0] - E - 1, width), F32)


def middle(scalars, pieces, grad_own, hown, gates, b, gains, router):
    rows, width = grad_own.shape
    operands = [*pieces, grad_own, hown, gates, b, gains, router]
    return pl.pallas_call(
        lambda *refs: middle_kernel(len(pieces), *refs),
        grid_spec=pltpu.PrefetchScalarGridSpec(
            num_scalar_prefetch=1,
            grid=(1,),
            in_specs=[whole(x.shape) for x in operands],
            out_specs=[whole((rows, width)), whole((rows, width)), whole((24, width))],
        ),
        out_shape=[
            jax.ShapeDtypeStruct((rows, width), F32),
            jax.ShapeDtypeStruct((rows, width), BF),
            jax.ShapeDtypeStruct((24, width), F32),
        ],
        compiler_params=params(),
        cost_estimate=pl.CostEstimate(
            flops=rows * width * 64, bytes_accessed=rows * width * 24, transcendentals=rows
        ),
        name="norm_backward",
    )(scalars, *operands)


def attention_backward_kernel(peers, sref, *refs):
    pieces, refs = refs[:peers], refs[peers:]
    (
        dh_ref,
        xown_ref,
        gains_ref,
        cos_ref,
        sin_ref,
        bias_ref,
        qkv_ref,
        lse_ref,
        w_ref,
        dx_ref,
        dxlow_ref,
        gain_ref,
        full_ref,
        dqkv_ref,
        total,
        now,
    ) = refs
    step = pl.program_id(0)
    me = sref[0]
    group, width = full_ref.shape
    shard = dh_ref.shape[0]

    @pl.when(step == 0)
    def _():
        assemble(me, pieces, peers, full_ref)
        total[...] = jnp.zeros_like(total)

    weights = w_ref[:, 0].reshape(width, -1)
    do = dot(full_ref[...], weights[:, 512:]).astype(BF)
    qkv = qkv_ref[0]
    q, k, v = qkv[:, :256], qkv[:, 256:384], qkv[:, 384:]
    q_turned = q.T
    do_turned = do.T
    bias = bias_ref[0]
    lse = lse_ref[0]
    dq, dk, dv = [], [], []
    for kv in range(2):
        k_one = k[:, kv * HD : (kv + 1) * HD]
        v_one = v[:, kv * HD : (kv + 1) * HD]
        dk_one = dv_one = None
        for head in (2 * kv, 2 * kv + 1):
            part = slice(head * HD, (head + 1) * HD)
            scores = dot_nt(q[:, part], k_one) + bias
            soft = jnp.exp(scores - lse[:, head : head + 1])
            grad_soft = dot_nt(do[:, part], v_one)
            grad_scores = soft * (
                grad_soft - jnp.sum(soft * grad_soft, axis=1, keepdims=True)
            )
            grad_scores = grad_scores.astype(BF)
            dq.append(dot(grad_scores, k_one))
            dk_part = dot(q_turned[part, :], grad_scores)
            dv_part = dot(do_turned[part, :], soft.astype(BF))
            dk_one = dk_part if dk_one is None else dk_one + dk_part
            dv_one = dv_part if dv_one is None else dv_one + dv_part
        dk.append(dk_one)
        dv.append(dv_one)
    grad_k = jnp.concatenate(dk, axis=0).T
    grad_v = jnp.concatenate(dv, axis=0).T
    grad_qk = jnp.concatenate([jnp.concatenate(dq, axis=1) * HD**-0.5, grad_k], axis=1)
    cos = jnp.concatenate([cos_ref[0]] * 3, axis=1)
    sin = jnp.concatenate([sin_ref[0]] * 3, axis=1)
    grad_qk = (grad_qk * cos - swap_halves(grad_qk) * sin).astype(BF)
    now[:, :384] = grad_qk
    now[:, 384:] = grad_v.astype(BF)

    @pl.when(step == me)
    def _():
        dqkv_ref[...] = now[...]

    total[...] += dot_nt(now[own_rows(me, shard), :], weights[:, :512])

    @pl.when(step == pl.num_programs(0) - 1)
    def _():
        entering = xown_ref[...].astype(F32)
        part, grad_gain = norm_back(
            entering, rms_scale(entering), gains_ref[0:1, :], total[...]
        )
        grad_entering = dh_ref[...] + part
        dx_ref[...] = grad_entering
        dxlow_ref[...] = grad_entering.astype(BF)
        gain_ref[...] = jnp.broadcast_to(grad_gain, gain_ref.shape)


def attention_backward(scalars, pieces, dh, xown, gains, tables, qkv, lse, w_attn):
    dp, peers, dr, cols = w_attn.shape
    width = dp * dr
    group = qkv.shape[1]
    shard = group // peers
    cos, sin, bias = tables
    pick = lambda i, s: (s[1], 0, 0)
    per_step = lambda i, s: (i, 0, 0)
    return pl.pallas_call(
        lambda *refs: attention_backward_kernel(peers, *refs),
        grid_spec=pltpu.PrefetchScalarGridSpec(
            num_scalar_prefetch=1,
            grid=(peers,),
            in_specs=[whole(x.shape) for x in pieces]
            + [
                whole(dh.shape),
                whole(xown.shape),
                whole(gains.shape),
                pl.BlockSpec((1,) + cos.shape[1:], pick),
                pl.BlockSpec((1,) + sin.shape[1:], pick),
                pl.BlockSpec((1,) + bias.shape[1:], pick),
                pl.BlockSpec((1, group, 512), per_step),
                pl.BlockSpec((1, group, LANES), per_step),
                pl.BlockSpec((dp, 1, dr, cols), lambda i, s: (0, i, 0, 0)),
            ],
            out_specs=[
                whole((shard, width)),
                whole((shard, width)),
                whole((8, width)),
                whole((group, width)),
                whole((group, 512)),
            ],
            scratch_shapes=[pltpu.VMEM((shard, width), F32), pltpu.VMEM((group, 512), BF)],
        ),
        out_shape=[
            jax.ShapeDtypeStruct((shard, width), F32),
            jax.ShapeDtypeStruct((shard, width), BF),
            jax.ShapeDtypeStruct((8, width), F32),
            jax.ShapeDtypeStruct((group, width), BF),
            jax.ShapeDtypeStruct((group, 512), BF),
        ],
        compiler_params=params(),
        cost_estimate=pl.CostEstimate(
            flops=group * width * 1024 * 2 + 16 * 10 * group * group * HD,
            bytes_accessed=w_attn.size * 2 + 6 * group * width * 2,
            transcendentals=16 * group * group,
        ),
        name="attention_backward",
    )(scalars, *pieces, dh, xown, gains, cos, sin, bias, qkv, lse, w_attn)


def expert_weights_kernel(
    b0_ref, b1_ref, g0_ref, g1_ref, g2_ref, dgu0_ref, dgu1_ref, dgu2_ref,
    ga0_ref, ga1_ref, out_ref, bt_ref, gt_ref,
):
    group = b0_ref.shape[0]
    dp, _, _, dr, ff = out_ref.shape

    @pl.when(pl.program_id(0) == 0)
    def _():
        bt_ref[:, :group] = b0_ref[...].T
        bt_ref[:, group:] = b1_ref[...].T
        gt_ref[:, :group] = (g0_ref[...] + g2_ref[...]).T
        gt_ref[:, group:] = g1_ref[...].T

    bt = bt_ref[...]
    for j in range(PER):
        rows = jnp.concatenate([dgu0_ref[j] + dgu2_ref[j], dgu1_ref[j]], axis=0)
        grads = dot(bt, rows).astype(BF)
        out_ref[:, 0, j] = grads[:, :ff].reshape(dp, dr, ff)
        out_ref[:, 1, j] = grads[:, ff:].reshape(dp, dr, ff)
    rows = jnp.concatenate([ga0_ref[...], ga1_ref[...]], axis=0)
    grads = dot(gt_ref[...], rows).astype(BF)
    for j in range(PER):
        out_ref[:, 2, j] = grads[:, j * ff : (j + 1) * ff].reshape(dp, dr, ff)


def expert_weights(rows_b, grads, dgus, gas, dp, first, count):
    group, width = rows_b[0].shape
    _, _, ff2 = dgus[0].shape
    ff = ff2 // 2
    dr = width // dp
    base = first // PER
    square = pl.BlockSpec((group, width), lambda i: (0, 0))
    wide = pl.BlockSpec((PER, group, ff2), lambda i: (base + i, 0, 0))
    flat = pl.BlockSpec((group, PER * ff), lambda i: (0, base + i))
    return pl.pallas_call(
        expert_weights_kernel,
        grid=(count // PER,),
        in_specs=[square] * 5 + [wide] * 3 + [flat] * 2,
        out_specs=pl.BlockSpec((dp, 3, PER, dr, ff), lambda i: (0, 0, i, 0, 0)),
        out_shape=jax.ShapeDtypeStruct((dp, 3, count, dr, ff), BF),
        scratch_shapes=[pltpu.VMEM((width, 2 * group), BF), pltpu.VMEM((width, 2 * group), BF)],
        compiler_params=params(),
        cost_estimate=pl.CostEstimate(
            flops=4 * group * width * ff * 3 * count,
            bytes_accessed=dp * 3 * count * dr * ff * 2 + 9 * count * group * ff * 2,
            transcendentals=0,
        ),
        name="expert_weight_grads",
    )(*rows_b, *grads, *dgus, *gas)


def attention_weights_kernel(
    sref, a0_ref, a1_ref, o0_ref, o1_ref, f0_ref, f1_ref, f2_ref, d0_ref, d1_ref, d2_ref, out_ref
):
    dp, dr, _ = out_ref.shape
    first = dot_tn(a0_ref[...], d0_ref[...] + d2_ref[...]) + dot_tn(a1_ref[...], d1_ref[...])
    out_ref[:, :, :512] = first.astype(BF).reshape(dp, dr, 512)
    second = dot_tn(f0_ref[...] + f2_ref[...], o0_ref[0]) + dot_tn(f1_ref[...], o1_ref[0])
    out_ref[:, :, 512:] = second.astype(BF).reshape(dp, dr, 256)


def attention_weights(scalars, a_rows, o_rows, fulls, dqkvs, dp):
    group, width = a_rows[0].shape
    dr = width // dp
    own = pl.BlockSpec((1, group, 256), lambda i, s: (s[0], 0, 0))
    return pl.pallas_call(
        attention_weights_kernel,
        grid_spec=pltpu.PrefetchScalarGridSpec(
            num_scalar_prefetch=1,
            grid=(1,),
            in_specs=[whole((group, width))] * 2
            + [own] * 2
            + [whole((group, width))] * 3
            + [whole((group, 512))] * 3,
            out_specs=whole((dp, dr, 768)),
        ),
        out_shape=jax.ShapeDtypeStruct((dp, dr, 768), BF),
        compiler_params=params(),
        cost_estimate=pl.CostEstimate(
            flops=4 * group * width * 768,
            bytes_accessed=group * width * 14 + width * 768 * 2,
            transcendentals=0,
        ),
        name="attention_weight_grads",
    )(scalars, *a_rows, *o_rows, *fulls, *dqkvs)


def moved(array, peers, shift):
    return lax.ppermute(array, "tensor", [(i, (i + shift) % peers) for i in range(peers)])


def to_owner(pieces, peers):
    return [pieces[0]] + [moved(pieces[s], peers, s) for s in range(1, peers)]


def to_all(rows, peers):
    return [rows] + [moved(rows, peers, s) for s in range(1, peers)]


def across(rows, peers, up):
    start, end = (0, peers) if up else (peers, 0)
    return [
        lax.ppermute(
            rows,
            ("pipe", "tensor"),
            [(start + i, end + (i + s) % peers) for i in range(peers)],
        )
        for s in range(peers)
    ]


def tables_of(lengths, group):
    ends = jnp.cumsum(lengths)
    starts = ends - lengths
    index = jnp.arange(group, dtype=jnp.int32)
    inside = index[:, None] >= starts[None, :]
    start = jnp.max(jnp.where(inside, starts[None, :], 0), axis=1)
    position = (index - start).astype(F32)
    half = HD // 2
    freq = jnp.exp(jnp.arange(half, dtype=F32) * (-2.0 * math.log(10000.0) / HD))
    angle = position[:, None] * freq[None, :]
    cos, sin = jnp.cos(angle), jnp.sin(angle)
    visible = (index[None, :] <= index[:, None]) & (index[None, :] >= start[:, None])
    bias = jnp.where(visible, 0.0, MASKED).astype(F32)
    return (
        jnp.concatenate([cos, cos, cos, cos], axis=1),
        jnp.concatenate([-sin, sin, -sin, sin], axis=1),
        bias,
    )


def per_device(
    inputs, cotangent, doc_lengths, routes, norm_attn, w_query, w_key, w_value, w_out,
    w_router, norm_ffn, w_gate, w_up, w_down,
):
    section = lax.axis_index("pipe")
    first_section = section == 0
    me = lax.axis_index("tensor")
    peers = lax.axis_size("tensor")
    dp = lax.axis_size("dp")
    micro = inputs.shape[0]
    shard, width = inputs.shape[1:]
    group = shard * peers

    piece = jnp.concatenate([w_query[0], w_key[0], w_value[0], w_out[0].T], axis=1)
    w_attn = lax.all_gather(lax.all_gather(piece, "tensor", axis=0), "dp", axis=0)
    small = jnp.concatenate(
        [w_router[0], norm_attn[0][:, None], norm_ffn[0][:, None]], axis=1
    )
    small = lax.all_gather(small, ("dp", "tensor"), axis=0, tiled=True)
    router = small[:, :E]
    gains = small[:, E:].T.astype(F32)
    rows_in = lax.all_gather(inputs, "tensor", axis=1, tiled=True)
    rows_in = jnp.where(first_section, rows_in, jnp.zeros_like(rows_in))
    pieces_w = jnp.stack([w_gate[0], w_up[0], w_down[0].transpose(0, 2, 1)])
    w_experts = lax.all_gather(pieces_w, "dp", axis=0)
    own_cot = jnp.where(first_section, jnp.zeros_like(cotangent), cotangent)
    full_cot = lax.all_gather(own_cot, "tensor", axis=1, tiled=True)

    tables = jax.vmap(lambda lengths: tables_of(lengths, group))(doc_lengths[:, 0])
    ids = jnp.arange(E, dtype=jnp.int32)
    picked = jnp.any(routes[0][..., None] == ids, axis=2).astype(F32)

    outputs, saves = [], []
    received = None
    for tick in range(micro + 1):
        which = jnp.clip(tick - section, 0, micro - 1)
        scalars = jnp.stack([me, which]).astype(jnp.int32)
        pieces = received if received is not None else []
        full = rows_in[tick] if tick < micro else None
        a, xown, qkv, mixed, lse, hown, b, gates = attention_forward(
            scalars, pieces, full, gains, tables, picked, w_attn, router
        )
        *parts, gu = experts_forward(scalars, b, gates, w_experts, peers)
        parts = to_owner(parts, peers)
        result = hown
        for part in parts:
            result = result + part.astype(F32)
        sent = result.astype(BF)
        outputs.append(sent)
        saves.append((a, xown, qkv, mixed, lse, hown, b, gates, gu))
        if tick < micro:
            received = across(sent, peers, True)

    chosen = jax.tree.map(lambda x, y: jnp.where(first_section, x, y), saves[0], saves[2])
    kept = [saves[1], chosen, saves[1]]
    received = None
    grads_in, small_total, per_tick = [], None, []
    for tick in range(micro + 1):
        a, xown, qkv, mixed, lse, hown, b, gates, gu = kept[tick]
        which = jnp.clip(tick - 1 + section, 0, micro - 1)
        scalars = jnp.stack([me, which]).astype(jnp.int32)
        pieces = received if received is not None else []
        full = full_cot[tick] if tick < micro else None
        *parts, grad, dgu, ga = experts_backward(scalars, pieces, full, gates, gu, w_experts, peers)
        grad_own = None
        if tick < micro:
            grad_own = own_cot[tick]
        if pieces:
            grad_own = pieces[0] if grad_own is None else grad_own + pieces[0]
        parts = to_owner(parts, peers)
        dh, do, small_part = middle(scalars, parts, grad_own, hown, gates, b, gains, router)
        dx, dx_low, gain_part, do_full, dqkv = attention_backward(
            scalars, to_all(do, peers), dh, xown, gains, tables, qkv, lse, w_attn
        )
        grads_in.append(dx)
        if tick < micro:
            received = across(dx_low, peers, False)
        small_part = jnp.concatenate([small_part[: E + 1], gain_part[:1]], axis=0)
        small_total = small_part if small_total is None else small_total + small_part
        per_tick.append((grad, dgu, ga, do_full, dqkv))

    grad_rows, dgus, gas, fulls, dqkvs = ([t[i] for t in per_tick] for i in range(5))
    grad_experts = expert_weights(
        [kept[0][6], kept[1][6]], grad_rows, dgus, gas[:2], dp, 0, E
    )
    expert_sums = lax.psum_scatter(grad_experts, "dp", scatter_dimension=0, tiled=True)[0]
    grad_attn = attention_weights(
        scalars, [kept[0][0], kept[1][0]], [kept[0][3], kept[1][3]], fulls, dqkvs, dp
    )
    attn_sums = lax.psum_scatter(grad_attn, "dp", scatter_dimension=0, tiled=True)[0]
    small_sums = lax.psum_scatter(
        small_total.T, ("dp", "tensor"), scatter_dimension=0, tiled=True
    )
    expert_sums = expert_sums.astype(F32)
    attn_sums = attn_sums.astype(F32)
    cols_q, cols_k = w_query.shape[2], w_key.shape[2]
    section_rows = jnp.stack(
        [jnp.where(first_section, outputs[m], outputs[m + 1]) for m in range(micro)]
    )
    grad_in = jnp.stack(
        [jnp.where(first_section, grads_in[m + 1], grads_in[m]) for m in range(micro)]
    )
    return (
        section_rows[None],
        grad_in[None],
        small_sums[:, E + 1][None],
        attn_sums[:, :cols_q][None],
        attn_sums[:, cols_q : cols_q + cols_k][None],
        attn_sums[:, cols_q + cols_k : cols_q + 2 * cols_k][None],
        attn_sums[:, cols_q + 2 * cols_k :].T[None],
        small_sums[:, :E][None],
        small_sums[:, E][None],
        expert_sums[0][None],
        expert_sums[1][None],
        expert_sums[2].transpose(0, 2, 1)[None],
    )


def solution(mesh):
    in_specs = (
        P(None, ("dp", "tensor"), None),
        P(None, ("dp", "tensor"), None),
        P(None, "dp", None),
        P("pipe", None, "dp", None),
        P("pipe", ("dp", "tensor")),
        P("pipe", "dp", "tensor"),
        P("pipe", "dp", "tensor"),
        P("pipe", "dp", "tensor"),
        P("pipe", "tensor", "dp"),
        P("pipe", ("dp", "tensor"), None),
        P("pipe", ("dp", "tensor")),
        P("pipe", None, "dp", "tensor"),
        P("pipe", None, "dp", "tensor"),
        P("pipe", None, "tensor", "dp"),
    )
    out_specs = (
        P("pipe", None, ("dp", "tensor"), None),
        P("pipe", None, ("dp", "tensor"), None),
        P("pipe", ("dp", "tensor")),
        P("pipe", "dp", "tensor"),
        P("pipe", "dp", "tensor"),
        P("pipe", "dp", "tensor"),
        P("pipe", "tensor", "dp"),
        P("pipe", ("dp", "tensor"), None),
        P("pipe", ("dp", "tensor")),
        P("pipe", None, "dp", "tensor"),
        P("pipe", None, "dp", "tensor"),
        P("pipe", None, "tensor", "dp"),
    )
    return jax.shard_map(
        per_device, mesh=mesh, in_specs=in_specs, out_specs=out_specs, check_vma=False
    )
```

time: 1930 us -> 936 us (0.48)
  blocking collectives: 657 us -> 156 us
  local copies, waits for them, and re-layouts: 304 us -> 24.4 us
  Pallas kernels: 0 us -> 189 us
  matrix products: 186 us -> 0 us
  waiting for transfers between devices: 613 us -> 446 us
  other arithmetic: 121 us -> 28.1 us
  starting transfers between devices: 15 us -> 66.1 us
    reduce_scatter x20 -> x2, waiting for transfers between devices: 605 us -> 140 us  [the longest x1 81.3 us: per_device(): lax.psum_scatter(grad_experts, 'dp', scatter_dimension=0, tiled=True)[0]]
    unnamed x2 -> x0, blocking collectives: 287 us -> none
    unnamed x29 -> x8, waiting for transfers between devices: 1.49 us -> 256 us
    all_gather x17 -> x2, blocking collectives: 370 us -> 156 us  [the longest x1 142 us: per_device(): small = lax.all_gather(small, ('dp', 'tensor'), axis=0, tiled=True)]
    gather x18 -> x0, local copies, waits for them, and re-layouts: 214 us -> none  [the longest x6 53.5 us: expert_rows(): return padded[source].reshape(E, capacity, full_rows.shape[1])]
    pallas_call x0 -> x17, Pallas kernels: none -> 189 us  [the longest x3 45.1 us: attention_backward(): pl.pallas_call(lambda *refs: attention_backward_kernel(peers, *refs), gri...]
    dot_general x90 -> x0, matrix products: 186 us -> none  [the longest x3 20.8 us: layer_forward(): jnp.einsum('ecf,efd->ecd', activated, weight_down, preferred_element_type...]
    ppermute x4 -> x43, starting transfers between devices: 12.7 us -> 65.6 us  [the longest x27 34.4 us: moved(): lax.ppermute(array, 'tensor', [(i, (i + shift) % peers) for i in range(pe...]
  transfers between devices with their start and end apart: 30 -> 50, of which waited for: 12 -> 26; matrix products, arithmetic and copies ran while one was open for 22% -> 4% of each run, Pallas kernels for 0% -> 9%
where the time goes in v1:
time: 936 us; the launch traced here: 925 us
  waiting for transfers between devices  446 us (48%)
  Pallas kernels  189 us (20%)
  blocking collectives  156 us (17%)
  starting transfers between devices  66.1 us (7%)
  other arithmetic  28.1 us (3%)
  local copies, waits for them, and re-layouts  24.4 us (3%)
  between operations  15.3 us (2%)
    unnamed x8, waiting for transfers between devices  256 us
    all_gather x1, blocking collectives, per_device(): small = lax.all_gather(small, ('dp', 'tensor'), axis=0, tiled=True)  142 us
    reduce_scatter x1, waiting for transfers between devices, per_device(): lax.psum_scatter(grad_experts, 'dp', scatter_dimension=0, tiled=True)[0]  81.3 us
    reduce_scatter x1, waiting for transfers between devices, per_device(): lax.psum_scatter(grad_attn, 'dp', scatter_dimension=0, tiled=True)[0]  58.3 us
    pallas_call x3, Pallas kernels, attention_backward(): pl.pallas_call(lambda *refs: attention_backward_kernel(peers, *refs), gri...  45.1 us
    pallas_call x3, Pallas kernels, experts_backward(): pl.pallas_call(lambda *refs: experts_backward_kernel(peers, len(given), f...  42.9 us
    pallas_call x3, Pallas kernels, experts_forward(): pl.pallas_call(lambda *refs: experts_forward_kernel(peers, *refs), grid_s...  36.2 us
    pallas_call x3, Pallas kernels, attention_forward(): pl.pallas_call(lambda *refs: attention_forward_kernel(len(pieces), full i...  35.2 us
  transfers between devices with their start and end apart: 50, of which 26 were waited for; matrix products, arithmetic and copies ran while one was open for 4% of the time, Pallas kernels for 9%

profile of v1, /device:TPU:0, one launch (start us, length us, event | category | flops | bytes accessed | tf_op | source)
XLA Modules:
  0.0 925.1 jit_solution(5760916479793627251)
XLA Ops:
  8.8 13.8 %all-gather = bf16[256,768]{1,0:T(8,128)(2,1)} all-gather(bf16[64,768]{1,0:T(8,128)(2,1)S(1)} %pad_maximum_fusion.3), channel_id=2, replica_groups=mesh['pipe'=2,'dp'=16,'tensor'=4] {'tensor'}, dimensions={0}, use_global_device_ids=true | all-gather | bytes 491520 | tf_op jit(solution)/shard_map/all_gather | solution.py:742
  29.1 142.2 %all_gather.28 = bf16[1024,18]{1,0:T(8,128)(2,1)S(1)} all-gather(bf16[16,18]{1,0:T(8,128)(2,1)S(1)} %pad_maximum_fusion.4), channel_id=1, replica_groups=mesh['pipe'=2,'dp'=16,'tensor'=4] {'dp','tensor'}, dimensions={0}, use_global_device_ids=true | all-gather | bytes 37440 | tf_op jit(solution)/shard_map/all_gather | solution.py:746
  178.4 11.7 %attention_forward.3 = (bf16[256,1024]{1,0:T(8,128)(2,1)}, bf16[64,1024]{1,0:T(8,128)(2,1)}, bf16[4,256,512]{2,1,0:T(8,128)(2,1)}, bf16[4,256,256]{2,1,0:T(8,128...) custom-call(s32[2]{0:T(128)} %pad_add_fusion.refs_0_, ...), custom_call_target="tpu_custom_call" | custom-call | flops 1879048192 | bytes 9437184 | tf_op jit(solution)/shard_map/attention_forward/pallas_call | solution.py:212
  190.1 12.0 %experts_forward.3 = (bf16[64,1024]{1,0:T(8,128)(2,1)}, bf16[64,1024]{1,0:T(8,128)(2,1)}, bf16[64,1024]{1,0:T(8,128)(2,1)}, bf16[64,1024]{1,0:T(8,128)(2,1)}, bf16[16,256,256]{2,1,0:T(8,128)(2,1)}) custom-call(s32[2]{0:T(128)} %pad_add_fusion.refs_0_, bf16[256,1024]{1,0:T(8,128)(2,1)} %get-tuple-element.95.refs_1_, f32[256,16]{1,0:T(8,128)} %get-tuple-element.96.refs_2_, ...), custom_call_target="tpu_custom_call" | custom-call | flops 3221225472 | bytes 14680064 | tf_op jit(solution)/shard_map/experts_forward/pallas_call | solution.py:272
  212.3 5.4 collective-permute-start.6
  225.6 11.9 %attention_forward.4 = (bf16[256,1024]{1,0:T(8,128)(2,1)}, bf16[64,1024]{1,0:T(8,128)(2,1)}, bf16[4,256,512]{2,1,0:T(8,128)(2,1)}, bf16[4,256,256]{2,1,0:T(8,128...) custom-call(s32[2]{0:T(128)} %pad_add_fusion.1.refs_0_, ...), custom_call_target="tpu_custom_call" | custom-call | flops 1879048192 | bytes 9437184 | tf_op jit(solution)/shard_map/attention_forward/pallas_call | solution.py:212
  237.5 12.0 %experts_forward.4 = (bf16[64,1024]{1,0:T(8,128)(2,1)}, bf16[64,1024]{1,0:T(8,128)(2,1)}, bf16[64,1024]{1,0:T(8,128)(2,1)}, bf16[64,1024]{1,0:T(8,128)(2,1)}, bf16[16,256,256]{2,1,0:T(8,128)(2,1)}) custom-call(s32[2]{0:T(128)} %pad_add_fusion.1.refs_0_, bf16[256,1024]{1,0:T(8,128)(2,1)} %get-tuple-element.102.refs_1_.refs_8_.b0_ref, ...), custom_call_target="tpu_custom_call" | custom-call | flops 3221225472 | bytes 14680064 | tf_op jit(solution)/shard_map/experts_forward/pallas_call | solution.py:272
  254.6 14.2 %experts_backward.3 = (bf16[64,1152]{1,0:T(8,128)(2,1)}, bf16[64,1152]{1,0:T(8,128)(2,1)}, bf16[64,1152]{1,0:T(8,128)(2,1)}, bf16[64,1152]{1,0:T(8,128)(2,1)}, b...) custom-call(s32[2]{0:T(128)} %pad_add_fusion.4.refs_0_, ...), custom_call_target="tpu_custom_call" | custom-call | flops 3221225472 | bytes 17825792 | tf_op jit(solution)/shard_map/experts_backward/pallas_call | solution.py:374
  272.8 6.3 collective-permute-start.13
  294.3 11.7 %attention_forward.5 = (bf16[256,1024]{1,0:T(8,128)(2,1)}, bf16[64,1024]{1,0:T(8,128)(2,1)}, bf16[4,256,512]{2,1,0:T(8,128)(2,1)}, bf16[4,256,256]{2,1,0:T(8,128...) custom-call(s32[2]{0:T(128)} %pad_add_fusion.2.refs_0_, ...), custom_call_target="tpu_custom_call" | custom-call | flops 1879048192 | bytes 9437184 | tf_op jit(solution)/shard_map/attention_forward/pallas_call | solution.py:212
  306.9 12.2 %experts_forward.5 = (bf16[64,1024]{1,0:T(8,128)(2,1)}, bf16[64,1024]{1,0:T(8,128)(2,1)}, bf16[64,1024]{1,0:T(8,128)(2,1)}, bf16[64,1024]{1,0:T(8,128)(2,1)}, bf16[16,256,256]{2,1,0:T(8,128)(2,1)}) custom-call(s32[2]{0:T(128)} %pad_add_fusion.2.refs_0_, bf16[256,1024]{1,0:T(8,128)(2,1)} %get-tuple-element.109.refs_1_, f32[256,16]{1,0:T(8,128)} %get-tuple-element.110.refs_2_, ...), custom_call_target="tpu_custom_call" | custom-call | flops 3221225472 | bytes 14680064 | tf_op jit(solution)/shard_map/experts_forward/pallas_call | solution.py:272
  325.0 15.1 %attention_backward.3 = (f32[64,1024]{1,0:T(8,128)}, bf16[64,1024]{1,0:T(8,128)(2,1)}, f32[8,1024]{1,0:T(8,128)}, bf16[256,1024]{1,0:T(8,128)(2,1)}, bf16[256,512]{1,0:T(8,128)(2,1)}) custom-call(s32[2]{0:T(128)} %pad_add_fusion.4.refs_0_, bf16[64,1024]{1,0:T(8,128)(2,1)} %get-tuple-element.120.refs_1_, bf16[64,1024]{1,0:T(8,128)(2,1)} %copy-done.38, ...), custom_call_target="tpu_custom_call" | custom-call | flops 1207959552 | bytes 9437184 | tf_op jit(solution)/shard_map/attention_backward/pallas_call | solution.py:553
  349.5 3.9 collective-permute-done.25.refs_3_
  356.9 14.5 %experts_backward.4 = (bf16[64,1152]{1,0:T(8,128)(2,1)}, bf16[64,1152]{1,0:T(8,128)(2,1)}, bf16[64,1152]{1,0:T(8,128)(2,1)}, bf16[64,1152]{1,0:T(8,128)(2,1)}, b...) custom-call(s32[2]{0:T(128)} %pad_add_fusion.3.refs_0_, ...), custom_call_target="tpu_custom_call" | custom-call | flops 3221225472 | bytes 17825792 | tf_op jit(solution)/shard_map/experts_backward/pallas_call | solution.py:374
  397.1 15.0 %attention_backward.4 = (f32[64,1024]{1,0:T(8,128)}, bf16[64,1024]{1,0:T(8,128)(2,1)}, f32[8,1024]{1,0:T(8,128)}, bf16[256,1024]{1,0:T(8,128)(2,1)}, bf16[256,512]{1,0:T(8,128)(2,1)}) custom-call(s32[2]{0:T(128)} %pad_add_fusion.3.refs_0_, bf16[64,1024]{1,0:T(8,128)(2,1)} %get-tuple-element.132.refs_1_, bf16[64,1024]{1,0:T(8,128)(2,1)} %copy-done.51, ...), custom_call_target="tpu_custom_call" | custom-call | flops 1207959552 | bytes 9437184 | tf_op jit(solution)/shard_map/attention_backward/pallas_call | solution.py:553
  427.8 14.1 %experts_backward.5 = (bf16[64,1152]{1,0:T(8,128)(2,1)}, bf16[64,1152]{1,0:T(8,128)(2,1)}, bf16[64,1152]{1,0:T(8,128)(2,1)}, bf16[64,1152]{1,0:T(8,128)(2,1)}, b...) custom-call(s32[2]{0:T(128)} %pad_add_fusion.5.refs_0_.sref, ...), custom_call_target="tpu_custom_call" | custom-call | flops 3221225472 | bytes 17825792 | tf_op jit(solution)/shard_map/experts_backward/pallas_call | solution.py:374
  445.5 4.0 collective-permute-done.37.refs_2_
  466.2 15.1 %attention_backward.5 = (f32[64,1024]{1,0:T(8,128)}, bf16[64,1024]{1,0:T(8,128)(2,1)}, f32[8,1024]{1,0:T(8,128)}, bf16[256,1024]{1,0:T(8,128)(2,1)}, bf16[256,512]{1,0:T(8,128)(2,1)}) custom-call(s32[2]{0:T(128)} %pad_add_fusion.5.refs_0_.sref, bf16[64,1024]{1,0:T(8,128)(2,1)} %get-tuple-element.147.refs_1_, bf16[64,1024]{1,0:T(8,128)(2,1)} %copy-done.47, ...), custom_call_target="tpu_custom_call" | custom-call | flops 1207959552 | bytes 9437184 | tf_op jit(solution)/shard_map/attention_backward/pallas_call | solution.py:553
  484.3 4.9 attention_weight_grads.1
  489.2 14.4 %expert_weight_grads.1 = bf16[16,3,16,64,128]{4,3,2,1,0:T(8,128)(2,1)} custom-call(bf16[256,1024]{1,0:T(8,128)(2,1)} %get-tuple-element.102.refs_1_.refs_8_.b0_ref, bf16[256,1024]{1,0:T(8,128)(2,1)} %broadcast_select_fusion.5.refs_8_.b1_ref, bf16[256,1024]{1,0:T(8,128)(2,1)} %get-tuple-element.168.g0_ref, bf16[256,1024]{1,0:T(8,128)(2,1)} %get-tuple-element.169.g1_ref, ...), custom_call_target="tpu_custom_call" | custom-call | flops 6442450944 | bytes 22020096 | tf_op jit(solution)/shard_map/expert_weight_grads/pallas_call | solution.py:631
  508.1 4.1 collective-permute-done.14
  514.7 255.4 %reduce-scatter.10.cloned.1.call-done = f32[16,18]{1,0:T(8,128)} async-done(((f32[1024,18]{1,0:T(8,128)}), f32[16,18]{1,0:T(8,128)}) %reduce-scatter.10.cloned.1.call-update) | async-done | bytes 1168
  773.5 58.3 %reduce-scatter.6.cloned.1.call-done = bf16[1,64,768]{2,1,0:T(8,128)(2,1)} async-done(((bf16[16,64,768]{2,1,0:T(8,128)(2,1)}), bf16[1,64,768]{2,1,0:T(8,128)(2,1)}) %reduce-scatter.6.cloned.1.call-update) | async-done | bytes 98320 | tf_op jit(solution)/shard_map/reduce_scatter | solution.py:817
  834.0 81.3 %reduce-scatter.8.cloned.1.call-done = bf16[1,3,16,64,128]{4,3,2,1,0:T(8,128)(2,1)} async-done(((bf16[16,3,16,64,128]{4,3,2,1,0:T(8,128)(2,1)}), bf16[1,3,16,64,128]{4,3,2,1,0:T(8,128)(2,1)}) %reduce-scatter.8.cloned.1.call-update) | async-done | bytes 786448 | tf_op jit(solution)/shard_map/reduce_scatter | solution.py:813
  (305 shorter events, 156.5 us)
Async XLA Ops:
  7.2 168.9 %all-gather.8.cloned.1.call-start = ((), (), s32[]{:S(2)}) async-start(), calls=%async_computation.3 | async-start | bytes 1310720 | tf_op jit(solution)/shard_map/all_gather | solution.py:749
  7.9 170.5 %all-gather.12.cloned.1.call-start = ((), (), s32[]{:S(2)}) async-start(), calls=%async_computation.7 | async-start | bytes 6684672 | tf_op jit(solution)/shard_map/all_gather | solution.py:742
  22.7 167.4 %all-gather.14.cloned.1.call-start = ((), (), s32[]{:S(2)}) async-start(), calls=%async_computation.8 | async-start | bytes 13369344 | tf_op jit(solution)/shard_map/all_gather | solution.py:752
  24.9 196.7 %all-gather.10.cloned.1.call-start = ((), (), s32[]{:S(2)}) async-start(), calls=%async_computation.4 | async-start | bytes 1310720 | tf_op jit(solution)/shard_map/all_gather | solution.py:754
  25.7 744.3 %reduce-scatter.10.cloned.1.call-start = ((), (), s32[]{:S(2)}) async-start(), calls=%async_computation.9 | async-start | bytes 532480
  212.3 11.6 %collective-permute-start.6 = (bf16[64,1024]{1,0:T(8,128)(2,1)S(1)}, bf16[64,1024]{1,0:T(8,128)(2,1)S(1)}, u32[]{:S(2)}, u32[]{:S(2)}) collective-permute-start(bf16[64,1024]{1,0:T(8,128)(2,1)S(1)} %add_convert_fusion.2), channel_id=1, source_target_pairs={{0,67},{1,64},{2,65},{3,66},{4,71},{5,68},{6,69},{7,70},{8,75},{9,... | collective-permute-start | bytes 393224 | tf_op jit(solution)/shard_map/ppermute | solution.py:699
  249.4 20.9 %collective-permute-start.7 = (bf16[64,1024]{1,0:T(8,128)(2,1)}, bf16[64,1024]{1,0:T(8,128)(2,1)S(1)}, u32[]{:S(2)}, u32[]{:S(2)}) collective-permute-start(bf16[64,1024]{1,0:T(8,128)(2,1)} %get-tuple-element.105), channel_id=1, source_target_pairs={{0,1},{1,2},{2,3},{3,0},{4,5},{5,6},{6,7},{7,4},{8,9},{9,10},{10,1... | collective-permute-start | bytes 393224 | tf_op jit(solution)/shard_map/ppermute | solution.py:685
  250.3 22.4 %collective-permute-start.8 = (bf16[64,1024]{1,0:T(8,128)(2,1)}, bf16[64,1024]{1,0:T(8,128)(2,1)S(1)}, u32[]{:S(2)}, u32[]{:S(2)}) collective-permute-start(bf16[64,1024]{1,0:T(8,128)(2,1)} %get-tuple-element.106), channel_id=1, source_target_pairs={{0,2},{1,3},{2,0},{3,1},{4,6},{5,7},{6,4},{7,5},{8,10},{9,11},{10,... | collective-permute-start | bytes 393224 | tf_op jit(solution)/shard_map/ppermute | solution.py:685
  253.0 19.6 %collective-permute-start.9 = (bf16[64,1024]{1,0:T(8,128)(2,1)}, bf16[64,1024]{1,0:T(8,128)(2,1)S(1)}, u32[]{:S(2)}, u32[]{:S(2)}) collective-permute-start(bf16[64,1024]{1,0:T(8,128)(2,1)} %get-tuple-element.107), channel_id=1, source_target_pairs={{0,3},{1,0},{2,1},{3,2},{4,7},{5,4},{6,5},{7,6},{8,11},{9,8},{10,9... | collective-permute-start | bytes 393224 | tf_op jit(solution)/shard_map/ppermute | solution.py:685
  268.8 13.0 %collective-permute-start.17 = (bf16[64,1152]{1,0:T(8,128)(2,1)}, bf16[64,1152]{1,0:T(8,128)(2,1)S(1)}, u32[]{:S(2)}, u32[]{:S(2)}) collective-permute-start(bf16[64,1152]{1,0:T(8,128)(2,1)} %get-tuple-element.117), channel_id=1, source_target_pairs={{0,1},{1,2},{2,3},{3,0},{4,5},{5,6},{6,7},{7,4},{8,9},{9,10},{10,1... | collective-permute-start | bytes 442376 | tf_op jit(solution)/shard_map/ppermute | solution.py:685
  269.5 13.6 %collective-permute-start.18 = (bf16[64,1152]{1,0:T(8,128)(2,1)}, bf16[64,1152]{1,0:T(8,128)(2,1)S(1)}, u32[]{:S(2)}, u32[]{:S(2)}) collective-permute-start(bf16[64,1152]{1,0:T(8,128)(2,1)} %get-tuple-element.118), channel_id=1, source_target_pairs={{0,2},{1,3},{2,0},{3,1},{4,6},{5,7},{6,4},{7,5},{8,10},{9,11},{10,... | collective-permute-start | bytes 442376 | tf_op jit(solution)/shard_map/ppermute | solution.py:685
  270.3 15.3 %collective-permute-start.19 = (bf16[64,1152]{1,0:T(8,128)(2,1)}, bf16[64,1152]{1,0:T(8,128)(2,1)S(1)}, u32[]{:S(2)}, u32[]{:S(2)}) collective-permute-start(bf16[64,1152]{1,0:T(8,128)(2,1)} %get-tuple-element.119), channel_id=1, source_target_pairs={{0,3},{1,0},{2,1},{3,2},{4,7},{5,4},{6,5},{7,6},{8,11},{9,8},{10,9... | collective-permute-start | bytes 442376 | tf_op jit(solution)/shard_map/ppermute | solution.py:685
  272.8 19.3 %collective-permute-start.13 = (bf16[64,1024]{1,0:T(8,128)(2,1)S(1)}, bf16[64,1024]{1,0:T(8,128)(2,1)S(1)}, u32[]{:S(2)}, u32[]{:S(2)}) collective-permute-start(bf16[64,1024]{1,0:T(8,128)(2,1)S(1)} %get-tuple-element.213), channel_id=1, source_target_pairs={{0,67},{1,64},{2,65},{3,66},{4,71},{5,68},{6,69},{7,70},{8,75},{9,... | collective-permute-start | bytes 393224 | tf_op jit(solution)/shard_map/ppermute | solution.py:699
  279.0 13.0 %collective-permute-start.12 = (bf16[64,1024]{1,0:T(8,128)(2,1)S(1)}, bf16[64,1024]{1,0:T(8,128)(2,1)S(1)}, u32[]{:S(2)}, u32[]{:S(2)}) collective-permute-start(bf16[64,1024]{1,0:T(8,128)(2,1)S(1)} %get-tuple-element.213), channel_id=1, source_target_pairs={{0,66},{1,67},{2,64},{3,65},{4,70},{5,71},{6,68},{7,69},{8,74},{9,... | collective-permute-start | bytes 393224 | tf_op jit(solution)/shard_map/ppermute | solution.py:699
  281.8 11.2 %collective-permute-start.11 = (bf16[64,1024]{1,0:T(8,128)(2,1)S(1)}, bf16[64,1024]{1,0:T(8,128)(2,1)S(1)}, u32[]{:S(2)}, u32[]{:S(2)}) collective-permute-start(bf16[64,1024]{1,0:T(8,128)(2,1)S(1)} %get-tuple-element.213), channel_id=1, source_target_pairs={{0,65},{1,66},{2,67},{3,64},{4,69},{5,70},{6,71},{7,68},{8,73},{9,... | collective-permute-start | bytes 393224 | tf_op jit(solution)/shard_map/ppermute | solution.py:699
  289.6 34.7 %collective-permute-start.22 = (bf16[64,1024]{1,0:T(8,128)(2,1)}, bf16[64,1024]{1,0:T(8,128)(2,1)S(1)}, u32[]{:S(2)}, u32[]{:S(2)}) collective-permute-start(bf16[64,1024]{1,0:T(8,128)(2,1)} %get-tuple-element.120.refs_1_), channel_id=1, source_target_pairs={{0,3},{1,0},{2,1},{3,2},{4,7},{5,4},{6,5},{7,6},{8,11},{9,8},{10,9... | collective-permute-start | bytes 393224 | tf_op jit(solution)/shard_map/ppermute | solution.py:685
  292.0 32.2 %collective-permute-start.21 = (bf16[64,1024]{1,0:T(8,128)(2,1)}, bf16[64,1024]{1,0:T(8,128)(2,1)S(1)}, u32[]{:S(2)}, u32[]{:S(2)}) collective-permute-start(bf16[64,1024]{1,0:T(8,128)(2,1)} %get-tuple-element.120.refs_1_), channel_id=1, source_target_pairs={{0,2},{1,3},{2,0},{3,1},{4,6},{5,7},{6,4},{7,5},{8,10},{9,11},{10,... | collective-permute-start | bytes 393224 | tf_op jit(solution)/shard_map/ppermute | solution.py:685
  292.0 32.2 %collective-permute-start.20 = (bf16[64,1024]{1,0:T(8,128)(2,1)}, bf16[64,1024]{1,0:T(8,128)(2,1)S(1)}, u32[]{:S(2)}, u32[]{:S(2)}) collective-permute-start(bf16[64,1024]{1,0:T(8,128)(2,1)} %get-tuple-element.120.refs_1_), channel_id=1, source_target_pairs={{0,1},{1,2},{2,3},{3,0},{4,5},{5,6},{6,7},{7,4},{8,9},{9,10},{10,1... | collective-permute-start | bytes 393224 | tf_op jit(solution)/shard_map/ppermute | solution.py:685
  341.4 12.1 %collective-permute-start.25 = (bf16[64,1024]{1,0:T(8,128)(2,1)}, bf16[64,1024]{1,0:T(8,128)(2,1)S(1)}, u32[]{:S(2)}, u32[]{:S(2)}) collective-permute-start(bf16[64,1024]{1,0:T(8,128)(2,1)} %get-tuple-element.125), channel_id=1, source_target_pairs={{64,2},{65,3},{66,0},{67,1},{68,6},{69,7},{70,4},{71,5},{72,10},{7... | collective-permute-start | bytes 393224 | tf_op jit(solution)/shard_map/ppermute | solution.py:699
  342.7 12.8 %collective-permute-start.24 = (bf16[64,1024]{1,0:T(8,128)(2,1)}, bf16[64,1024]{1,0:T(8,128)(2,1)S(1)}, u32[]{:S(2)}, u32[]{:S(2)}) collective-permute-start(bf16[64,1024]{1,0:T(8,128)(2,1)} %get-tuple-element.125), channel_id=1, source_target_pairs={{64,1},{65,2},{66,3},{67,0},{68,5},{69,6},{70,7},{71,4},{72,9},{73... | collective-permute-start | bytes 393224 | tf_op jit(solution)/shard_map/ppermute | solution.py:699
  344.0 12.3 %collective-permute-start.23 = (bf16[64,1024]{1,0:T(8,128)(2,1)}, bf16[64,1024]{1,0:T(8,128)(2,1)S(1)}, u32[]{:S(2)}, u32[]{:S(2)}) collective-permute-start(bf16[64,1024]{1,0:T(8,128)(2,1)} %get-tuple-element.125), channel_id=1, source_target_pairs={{64,0},{65,1},{66,2},{67,3},{68,4},{69,5},{70,6},{71,7},{72,8},{73... | collective-permute-start | bytes 393224 | tf_op jit(solution)/shard_map/ppermute | solution.py:699
  416.0 11.2 %collective-permute-start.33 = (bf16[64,1024]{1,0:T(8,128)(2,1)}, bf16[64,1024]{1,0:T(8,128)(2,1)S(1)}, u32[]{:S(2)}, u32[]{:S(2)}) collective-permute-start(bf16[64,1024]{1,0:T(8,128)(2,1)} %get-tuple-element.142), channel_id=1, source_target_pairs={{64,0},{65,1},{66,2},{67,3},{68,4},{69,5},{70,6},{71,7},{72,8},{73... | collective-permute-start | bytes 393224 | tf_op jit(solution)/shard_map/ppermute | solution.py:699
  483.1 348.7 %reduce-scatter.6.cloned.1.call-start = ((), (), s32[]{:S(2)}) async-start(), calls=%async_computation.5 | async-start | bytes 1671168 | tf_op jit(solution)/shard_map/reduce_scatter | solution.py:817
  489.2 426.2 %reduce-scatter.8.cloned.1.call-start = ((), (), s32[]{:S(2)}) async-start(), calls=%async_computation.6 | async-start | bytes 13369344 | tf_op jit(solution)/shard_map/reduce_scatter | solution.py:813
  (97 other events, 750.5 us)
Sparse Core Ops, SparseCore 0:
  9.7 26.4 all-gather.7
  37.9 42.8 all-gather.11
  82.5 73.1 all-gather.13
  157.2 24.4 all-gather.9
  483.2 286.8 reduce-scatter.9
  772.4 59.3 reduce-scatter.5
  834.2 81.0 reduce-scatter.7

commit v2 on v1

v2 whole, which is shorter than its diff:
```python
import math

import jax
import jax.numpy as jnp
from jax import lax
from jax.experimental import pallas as pl
from jax.experimental.pallas import tpu as pltpu
from jax.sharding import PartitionSpec as P

HD = 64
E = 16
TOP = 8
EPSILON = 1e-06
MASKED = -1000000000.0
BF = jnp.bfloat16
F32 = jnp.float32
VMEM_LIMIT = 56 * 1024 * 1024
PER = 2
LANES = 128


def params():
    return pltpu.CompilerParams(
        vmem_limit_bytes=VMEM_LIMIT, dimension_semantics=("arbitrary",)
    )


def dot(left, right):
    return jnp.dot(left, right, preferred_element_type=F32)


def dot_nt(left, right):
    return lax.dot_general(
        left, right, (((1,), (1,)), ((), ())), preferred_element_type=F32
    )


def dot_tn(left, right):
    return lax.dot_general(
        left, right, (((0,), (0,)), ((), ())), preferred_element_type=F32
    )


def column(rows, index):
    lanes = lax.broadcasted_iota(jnp.int32, rows.shape, 1)
    return jnp.sum(jnp.where(lanes == index, rows, 0.0), axis=1, keepdims=True)


def whole(shape):
    return pl.BlockSpec(shape, lambda i, s: (0,) * len(shape))


def rms_scale(values):
    return lax.rsqrt(jnp.mean(values * values, axis=-1, keepdims=True) + EPSILON)


def norm_back(values, scale_rows, gain, grad_normed):
    weighted = grad_normed * gain
    grad_values = scale_rows * weighted - values * scale_rows**3 * jnp.mean(
        weighted * values, axis=-1, keepdims=True
    )
    grad_gain = jnp.sum(grad_normed * values * scale_rows, axis=0, keepdims=True)
    return grad_values, grad_gain


def swap_halves(values):
    width = values.shape[1]
    lanes = lax.broadcasted_iota(jnp.int32, values.shape, 1)
    ahead = pltpu.roll(values, width - HD // 2, 1)
    behind = pltpu.roll(values, HD // 2, 1)
    return jnp.where(lanes % HD < HD // 2, ahead, behind)


def assemble(me, pieces, target):
    rows = pieces[0].shape[0]
    for shift in range(4):
        owner = lax.rem(me + 4 - shift, 4)
        target[own_rows(owner, rows), :] = pieces[shift][...]


def own_rows(me, rows):
    return pl.ds(pl.multiple_of(me * rows, rows), rows)


def anywhere(count):
    return [pl.BlockSpec(memory_space=pl.ANY)] * count


def fetches(sources, buffers, sems):
    copies = []
    for shift in range(4):
        if shift == 2:
            half = sources[2].shape[0]
            copies.append(
                [
                    pltpu.make_async_copy(sources[2], buffers.at[2, pl.ds(0, half)], sems.at[2]),
                    pltpu.make_async_copy(
                        sources[3], buffers.at[2, pl.ds(half, half)], sems.at[4]
                    ),
                ]
            )
        else:
            source = sources[shift] if shift < 2 else sources[4]
            copies.append(
                [pltpu.make_async_copy(source, buffers.at[shift], sems.at[shift])]
            )
    return copies


def group_weights(buffers, step):
    dp = buffers.shape[1]
    blocks = [
        buffers[step, :, 64 * j : 64 * (j + 1), :].reshape(dp * 64, LANES) for j in range(6)
    ]
    return jnp.concatenate(blocks[:4], axis=1), jnp.concatenate(blocks[4:], axis=1)


def smalls_kernel(sref, *refs):
    sources, (router_ref, gains_ref, stage, sems) = refs[:5], refs[5:]
    dp = stage.shape[0]
    half = dp // 2
    me = sref[0]
    copies = []
    for place, source in enumerate(sources):
        shift = (0, 1, 2, 2, 3)[place]
        owner = lax.rem(me + 4 - shift, 4)
        rows = pl.ds(0, dp)
        if shift == 2:
            rows = pl.ds(half * (place - 2), half)
        copies.append(
            pltpu.make_async_copy(
                source.at[:, pl.ds(384, 16)], stage.at[rows, owner], sems.at[place]
            )
        )
    for copy in copies:
        copy.start()
    for copy in copies:
        copy.wait()
    rows = stage[...].reshape(dp * 64, LANES)
    router_ref[...] = rows
    turned = rows.astype(F32).T
    gains_ref[...] = turned[E : E + 8, :]


def smalls_of(scalars, w_attn):
    dp = w_attn[0].shape[0]
    width = dp * 64
    return pl.pallas_call(
        smalls_kernel,
        grid_spec=pltpu.PrefetchScalarGridSpec(
            num_scalar_prefetch=1,
            grid=(1,),
            in_specs=anywhere(5),
            out_specs=[whole((width, LANES)), whole((8, width))],
            scratch_shapes=[pltpu.VMEM((dp, 4, 16, LANES), BF), pltpu.SemaphoreType.DMA((5,))],
        ),
        out_shape=[
            jax.ShapeDtypeStruct((width, LANES), BF),
            jax.ShapeDtypeStruct((8, width), F32),
        ],
        compiler_params=params(),
        name="router_and_gains",
    )(scalars, *w_attn)


def attention_forward_kernel(n_after, sref, *refs):
    pieces, refs = refs[:4], refs[4:]
    sources, refs = refs[:5], refs[5 + n_after :]
    (
        gains_ref, cos_ref, sin_ref, bias_ref, picked_ref, router_ref,
        a_ref, xown_ref, qkv_ref, o_ref, lse_ref, hown_ref, b_ref, gates_ref,
        hidden, buffers, sems,
    ) = refs
    step = pl.program_id(0)
    me = sref[0]
    group, width = b_ref.shape
    shard = xown_ref.shape[0]

    @pl.when(sref[1] > 0)
    def _():
        copies = fetches(sources, buffers, sems)

        @pl.when(step == 0)
        def _():
            for part in copies:
                for copy in part:
                    copy.start()
            assemble(me, pieces, b_ref)
            entering = b_ref[...].astype(F32)
            a_ref[...] = (entering * rms_scale(entering) * gains_ref[0:1, :]).astype(BF)
            xown_ref[...] = pieces[0][...]
            hidden[...] = entering

        for shift, part in enumerate(copies):

            @pl.when(step == shift)
            def _(part=part):
                for copy in part:
                    copy.wait()

        w_qkv, w_out = group_weights(buffers, step)
        qkv = dot(a_ref[...], w_qkv)
        qk = qkv[:, :384]
        cos = jnp.concatenate([cos_ref[...]] * 3, axis=1)
        sin = jnp.concatenate([sin_ref[...]] * 3, axis=1)
        turned = qk * cos + swap_halves(qk) * sin
        q = (turned[:, :256] * HD**-0.5).astype(BF)
        k = turned[:, 256:].astype(BF)
        v = qkv[:, 384:].astype(BF)
        qkv_ref[0, :, :256] = q
        qkv_ref[0, :, 256:384] = k
        qkv_ref[0, :, 384:] = v
        bias = bias_ref[...]
        lanes = lax.broadcasted_iota(jnp.int32, (group, LANES), 1)
        lse_all = jnp.zeros((group, LANES), F32)
        outs = []
        for head in range(4):
            kv = head // 2
            scores = dot_nt(q[:, head * HD : (head + 1) * HD], k[:, kv * HD : (kv + 1) * HD])
            scores = scores + bias
            peak = jnp.max(scores, axis=1, keepdims=True)
            soft = jnp.exp(scores - peak)
            total = jnp.sum(soft, axis=1, keepdims=True)
            lse_all = jnp.where(lanes == head, peak + jnp.log(total), lse_all)
            soft = (soft * (1.0 / total)).astype(BF)
            outs.append(dot(soft, v[:, kv * HD : (kv + 1) * HD]))
        mixed = jnp.concatenate(outs, axis=1).astype(BF)

        @pl.when(step == 0)
        def _():
            o_ref[...] = mixed

        lse_ref[0] = lse_all
        hidden[...] += dot_nt(mixed, w_out)

        @pl.when(step == pl.num_programs(0) - 1)
        def _():
            rows = hidden[...]
            normed = (rows * rms_scale(rows) * gains_ref[1:2, :]).astype(BF)
            b_ref[...] = normed
            hown_ref[...] = hidden[own_rows(me, shard), :]
            logits = dot(normed, router_ref[...])[:, :E]
            picked = picked_ref[...]
            peak = jnp.max(jnp.where(picked > 0, logits, -1e30), axis=1, keepdims=True)
            powers = jnp.where(picked > 0, jnp.exp(jnp.minimum(logits - peak, 0.0)), 0.0)
            gates_ref[...] = powers / jnp.sum(powers, axis=1, keepdims=True)


def attention_forward(scalars, pieces, gains, tables, picked, w_attn, router, after):
    shard, width = pieces[0].shape
    group = 4 * shard
    dp = width // 64
    cos, sin, bias = tables
    smalls = [gains, cos, sin, bias, picked, router]
    per_step = lambda i, s: (i * s[1], 0, 0)
    outs = [
        ((group, width), BF, None),
        ((shard, width), BF, None),
        ((4, group, 512), BF, (1, group, 512)),
        ((group, 256), BF, None),
        ((4, group, LANES), F32, (1, group, LANES)),
        ((shard, width), F32, None),
        ((group, width), BF, None),
        ((group, E), F32, None),
    ]
    return pl.pallas_call(
        lambda *refs: attention_forward_kernel(len(after), *refs),
        grid_spec=pltpu.PrefetchScalarGridSpec(
            num_scalar_prefetch=1,
            grid=(4,),
            in_specs=[whole(x.shape) for x in pieces]
            + anywhere(5 + len(after))
            + [whole(x.shape) for x in smalls],
            out_specs=[
                whole(shape) if block is None else pl.BlockSpec(block, per_step)
                for shape, _, block in outs
            ],
            scratch_shapes=[
                pltpu.VMEM((group, width), F32),
                pltpu.VMEM((4, dp, 400, LANES), BF),
                pltpu.SemaphoreType.DMA((5,)),
            ],
        ),
        out_shape=[jax.ShapeDtypeStruct(shape, kind) for shape, kind, _ in outs],
        compiler_params=params(),
        cost_estimate=pl.CostEstimate(
            flops=2 * group * width * 768 * 4 + 16 * 4 * group * group * HD,
            bytes_accessed=width * 768 * 8 + 6 * group * width * 2,
            transcendentals=16 * group * group,
        ),
        name="attention_forward",
    )(scalars, *pieces, *w_attn, *after, *smalls)


def experts_forward_kernel(n_after, sref, *refs):
    (b_ref, gate_ref, w_ref, *refs) = refs[n_after:]
    pieces, (gu_ref, total) = refs[:4], refs[4:]
    step = pl.program_id(0)
    width = b_ref.shape[1]
    ff = w_ref.shape[-1]

    @pl.when(sref[1] > 0)
    def _():
        b = b_ref[...]
        gates = gate_ref[...]
        acts, downs = [], []
        for j in range(PER):
            gate_up = jnp.concatenate(
                [w_ref[:, 0, j].reshape(width, ff), w_ref[:, 1, j].reshape(width, ff)], axis=1
            )
            both = dot(b, gate_up)
            gu_ref[j] = both.astype(BF)
            gate_pre, up_pre = both[:, :ff], both[:, ff:]
            act = gate_pre * jax.nn.sigmoid(gate_pre) * up_pre
            acts.append((act * column(gates, step * PER + j)).astype(BF))
            downs.append(w_ref[:, 2, j].reshape(width, ff))
        out = dot_nt(jnp.concatenate(acts, axis=1), jnp.concatenate(downs, axis=1))

        @pl.when(step == 0)
        def _():
            total[...] = out

        @pl.when(step > 0)
        def _():
            total[...] += out

        @pl.when(step == pl.num_programs(0) - 1)
        def _():
            rows = b_ref.shape[0] // 4
            for shift in range(4):
                place = own_rows(lax.rem(sref[0] + shift, 4), rows)
                pieces[shift][...] = total[place, :].astype(BF)


def experts_forward(scalars, b, gates, w, after):
    group, width = b.shape
    dp, _, experts, dr, ff = w.shape
    piece = (group // 4, width)
    return pl.pallas_call(
        lambda *refs: experts_forward_kernel(len(after), *refs),
        grid_spec=pltpu.PrefetchScalarGridSpec(
            num_scalar_prefetch=1,
            grid=(experts // PER,),
            in_specs=anywhere(len(after))
            + [
                whole((group, width)),
                whole((group, experts)),
                pl.BlockSpec((dp, 3, PER, dr, ff), lambda i, s: (0, 0, i * s[1], 0, 0)),
            ],
            out_specs=[whole(piece)] * 4
            + [pl.BlockSpec((PER, group, 2 * ff), lambda i, s: (i * s[1], 0, 0))],
            scratch_shapes=[pltpu.VMEM((group, width), F32)],
        ),
        out_shape=[jax.ShapeDtypeStruct(piece, BF)] * 4
        + [jax.ShapeDtypeStruct((experts, group, 2 * ff), BF)],
        compiler_params=params(),
        cost_estimate=pl.CostEstimate(
            flops=2 * group * width * ff * 3 * experts,
            bytes_accessed=w.size * 2 + experts * group * 2 * ff * 2,
            transcendentals=experts * group * ff,
        ),
        name="experts_forward",
    )(scalars, *after, b, gates, w)


def experts_backward_kernel(n_after, sref, *refs):
    (*refs,) = refs[n_after:]
    given, refs = refs[:4], refs[4:]
    gate_ref, gu_ref, w_ref, *refs = refs
    pieces, refs = refs[:4], refs[4:]
    grad_ref, dgu_ref, ga_ref, total, total_gate = refs
    step = pl.program_id(0)
    group, width = grad_ref.shape
    ff = w_ref.shape[-1]

    @pl.when(sref[1] > 0)
    def _():
        @pl.when(step == 0)
        def _():
            assemble(sref[0], given, grad_ref)

        grad = grad_ref[...]
        gates = gate_ref[...]
        down = jnp.concatenate(
            [w_ref[:, 2, j].reshape(width, ff) for j in range(PER)], axis=1
        )
        turned = dot(grad, down)
        lanes = lax.broadcasted_iota(jnp.int32, (group, LANES), 1)
        grad_gate = jnp.zeros((group, LANES), F32)
        out = None
        for j in range(PER):
            expert = step * PER + j
            back = turned[:, j * ff : (j + 1) * ff]
            both = gu_ref[j].astype(F32)
            gate_pre, up_pre = both[:, :ff], both[:, ff:]
            sigma = jax.nn.sigmoid(gate_pre)
            silu = gate_pre * sigma
            act = silu * up_pre
            gate = column(gates, expert)
            grad_gate = jnp.where(
                lanes == expert, jnp.sum(act * back, axis=1, keepdims=True), grad_gate
            )
            grad_act = gate * back
            grad_pre = grad_act * up_pre * sigma * (1.0 + gate_pre * (1.0 - sigma))
            grad_up = grad_act * silu
            grad_both = jnp.concatenate([grad_pre.astype(BF), grad_up.astype(BF)], axis=1)
            dgu_ref[j] = grad_both
            ga_ref[:, j * ff : (j + 1) * ff] = (gate * act).astype(BF)
            gate_up = jnp.concatenate(
                [w_ref[:, 0, j].reshape(width, ff), w_ref[:, 1, j].reshape(width, ff)], axis=1
            )
            part = dot_nt(grad_both, gate_up)
            out = part if out is None else out + part

        @pl.when(step == 0)
        def _():
            total[...] = out
            total_gate[...] = grad_gate

        @pl.when(step > 0)
        def _():
            total[...] += out
            total_gate[...] += grad_gate

        @pl.when(step == pl.num_programs(0) - 1)
        def _():
            rows = group // 4
            for shift in range(4):
                place = own_rows(lax.rem(sref[0] + shift, 4), rows)
                pieces[shift][:, :width] = total[place, :].astype(BF)
                pieces[shift][:, width:] = total_gate[place, :].astype(BF)


def experts_backward(scalars, given, gates, gu, w, after):
    dp, _, experts, dr, ff = w.shape
    group = gates.shape[0]
    width = dp * dr
    piece = (group // 4, width + LANES)
    return pl.pallas_call(
        lambda *refs: experts_backward_kernel(len(after), *refs),
        grid_spec=pltpu.PrefetchScalarGridSpec(
            num_scalar_prefetch=1,
            grid=(experts // PER,),
            in_specs=anywhere(len(after))
            + [whole(x.shape) for x in given]
            + [
                whole((group, experts)),
                pl.BlockSpec((PER, group, 2 * ff), lambda i, s: (i * s[1], 0, 0)),
                pl.BlockSpec((dp, 3, PER, dr, ff), lambda i, s: (0, 0, i * s[1], 0, 0)),
            ],
            out_specs=[whole(piece)] * 4
            + [
                whole((group, width)),
                pl.BlockSpec((PER, group, 2 * ff), lambda i, s: (i * s[1], 0, 0)),
                pl.BlockSpec((group, PER * ff), lambda i, s: (0, i * s[1])),
            ],
            scratch_shapes=[pltpu.VMEM((group, width), F32), pltpu.VMEM((group, LANES), F32)],
        ),
        out_shape=[jax.ShapeDtypeStruct(piece, BF)] * 4
        + [
            jax.ShapeDtypeStruct((group, width), BF),
            jax.ShapeDtypeStruct((experts, group, 2 * ff), BF),
            jax.ShapeDtypeStruct((group, experts * ff), BF),
        ],
        compiler_params=params(),
        cost_estimate=pl.CostEstimate(
            flops=2 * group * width * ff * 3 * experts,
            bytes_accessed=w.size * 2 + 5 * experts * group * ff * 2,
            transcendentals=experts * group * ff,
        ),
        name="experts_backward",
    )(scalars, *after, *given, gates, gu, w)


def middle_kernel(n_after, sref, *refs):
    refs = refs[n_after:]
    pieces, refs = refs[:4], refs[4:]
    grad_ref, hown_ref, gates_ref, b_ref, gains_ref, router_ref, dh_ref, do_ref, small_ref = refs
    rows, width = grad_ref.shape

    @pl.when(sref[1] > 0)
    def _():
        place = own_rows(sref[0], rows)
        joined = pieces[0][...].astype(F32)
        for shift in range(1, 4):
            joined = joined + pieces[shift][...].astype(F32)
        grad_normed = joined[:, :width]
        grad_gate = joined[:, width : width + E]
        gates = gates_ref[place, :]
        grad_logits = (
            gates * (grad_gate - jnp.sum(gates * grad_gate, axis=1, keepdims=True))
        ).astype(BF)
        normed = b_ref[place, :]
        grad_normed = grad_normed + dot_nt(grad_logits, router_ref[:, :E])
        hidden = hown_ref[...]
        part, grad_gain = norm_back(hidden, rms_scale(hidden), gains_ref[1:2, :], grad_normed)
        grad_hidden = grad_ref[...].astype(F32) + part
        dh_ref[...] = grad_hidden
        do_ref[...] = grad_hidden.astype(BF)
        small_ref[0:E, :] = dot_tn(grad_logits, normed)
        small_ref[E : E + 1, :] = grad_gain
        small_ref[E + 1 :, :] = jnp.zeros((small_ref.shape[0] - E - 1, width), F32)


def middle(scalars, pieces, grad_own, hown, gates, b, gains, router, after):
    rows, width = grad_own.shape
    operands = [*pieces, grad_own, hown, gates, b, gains, router]
    return pl.pallas_call(
        lambda *refs: middle_kernel(len(after), *refs),
        grid_spec=pltpu.PrefetchScalarGridSpec(
            num_scalar_prefetch=1,
            grid=(1,),
            in_specs=anywhere(len(after)) + [whole(x.shape) for x in operands],
            out_specs=[whole((rows, width)), whole((rows, width)), whole((24, width))],
        ),
        out_shape=[
            jax.ShapeDtypeStruct((rows, width), F32),
            jax.ShapeDtypeStruct((rows, width), BF),
            jax.ShapeDtypeStruct((24, width), F32),
        ],
        compiler_params=params(),
        cost_estimate=pl.CostEstimate(
            flops=rows * width * 64, bytes_accessed=rows * width * 24, transcendentals=rows
        ),
        name="norm_backward",
    )(scalars, *after, *operands)


def attention_backward_kernel(n_after, sref, *refs):
    pieces, refs = refs[:4], refs[4:]
    sources, refs = refs[:5], refs[5 + n_after :]
    (
        dh_ref, xown_ref, small_ref, gains_ref, cos_ref, sin_ref, bias_ref, qkv_ref, lse_ref,
        dx_ref, dxlow_ref, small_out_ref, full_ref, dqkv_ref,
        total, now, buffers, sems,
    ) = refs
    step = pl.program_id(0)
    me = sref[0]
    shard = dh_ref.shape[0]

    @pl.when(sref[1] > 0)
    def _():
        copies = fetches(sources, buffers, sems)

        @pl.when(step == 0)
        def _():
            for part in copies:
                for copy in part:
                    copy.start()
            assemble(me, pieces, full_ref)
            total[...] = jnp.zeros_like(total)

        for shift, part in enumerate(copies):

            @pl.when(step == shift)
            def _(part=part):
                for copy in part:
                    copy.wait()

        w_qkv, w_out = group_weights(buffers, step)
        do = dot(full_ref[...], w_out).astype(BF)
        qkv = qkv_ref[0]
        q, k, v = qkv[:, :256], qkv[:, 256:384], qkv[:, 384:]
        q_turned = q.T
        do_turned = do.T
        bias = bias_ref[...]
        lse = lse_ref[0]
        dq, dk, dv = [], [], []
        for kv in range(2):
            k_one = k[:, kv * HD : (kv + 1) * HD]
            v_one = v[:, kv * HD : (kv + 1) * HD]
            dk_one = dv_one = None
            for head in (2 * kv, 2 * kv + 1):
                part = slice(head * HD, (head + 1) * HD)
                scores = dot_nt(q[:, part], k_one) + bias
                soft = jnp.exp(scores - lse[:, head : head + 1])
                grad_soft = dot_nt(do[:, part], v_one)
                grad_scores = soft * (
                    grad_soft - jnp.sum(soft * grad_soft, axis=1, keepdims=True)
                )
                grad_scores = grad_scores.astype(BF)
                dq.append(dot(grad_scores, k_one))
                dk_part = dot(q_turned[part, :], grad_scores)
                dv_part = dot(do_turned[part, :], soft.astype(BF))
                dk_one = dk_part if dk_one is None else dk_one + dk_part
                dv_one = dv_part if dv_one is None else dv_one + dv_part
            dk.append(dk_one)
            dv.append(dv_one)
        grad_k = jnp.concatenate(dk, axis=0).T
        grad_v = jnp.concatenate(dv, axis=0).T
        grad_qk = jnp.concatenate([jnp.concatenate(dq, axis=1) * HD**-0.5, grad_k], axis=1)
        cos = jnp.concatenate([cos_ref[...]] * 3, axis=1)
        sin = jnp.concatenate([sin_ref[...]] * 3, axis=1)
        grad_qk = (grad_qk * cos - swap_halves(grad_qk) * sin).astype(BF)
        now[:, :384] = grad_qk
        now[:, 384:] = grad_v.astype(BF)

        @pl.when(step == 0)
        def _():
            dqkv_ref[...] = now[...]

        total[...] += dot_nt(now[own_rows(me, shard), :], w_qkv)

        @pl.when(step == pl.num_programs(0) - 1)
        def _():
            entering = xown_ref[...].astype(F32)
            part, grad_gain = norm_back(
                entering, rms_scale(entering), gains_ref[0:1, :], total[...]
            )
            grad_entering = dh_ref[...] + part
            dx_ref[...] = grad_entering
            dxlow_ref[...] = grad_entering.astype(BF)
            rows = lax.broadcasted_iota(jnp.int32, small_ref.shape, 0)
            small_out_ref[...] = jnp.where(rows == E + 1, grad_gain, small_ref[...])


def attention_backward(
    scalars, pieces, dh, xown, small, gains, tables, qkv, lse, w_attn, after
):
    shard, width = dh.shape
    group = 4 * shard
    dp = width // 64
    cos, sin, bias = tables
    smalls = [dh, xown, small, gains, cos, sin, bias]
    per_step = lambda i, s: (i * s[1], 0, 0)
    outs = [
        ((shard, width), F32),
        ((shard, width), BF),
        (small.shape, F32),
        ((group, width), BF),
        ((group, 512), BF),
    ]
    return pl.pallas_call(
        lambda *refs: attention_backward_kernel(len(after), *refs),
        grid_spec=pltpu.PrefetchScalarGridSpec(
            num_scalar_prefetch=1,
            grid=(4,),
            in_specs=[whole(x.shape) for x in pieces]
            + anywhere(5 + len(after))
            + [whole(x.shape) for x in smalls]
            + [
                pl.BlockSpec((1, group, 512), per_step),
                pl.BlockSpec((1, group, LANES), per_step),
            ],
            out_specs=[whole(shape) for shape, _ in outs],
            scratch_shapes=[
                pltpu.VMEM((shard, width), F32),
                pltpu.VMEM((group, 512), BF),
                pltpu.VMEM((4, dp, 400, LANES), BF),
                pltpu.SemaphoreType.DMA((5,)),
            ],
        ),
        out_shape=[jax.ShapeDtypeStruct(shape, kind) for shape, kind in outs],
        compiler_params=params(),
        cost_estimate=pl.CostEstimate(
            flops=group * width * 1024 * 2 + 16 * 10 * group * group * HD,
            bytes_accessed=width * 768 * 8 + 6 * group * width * 2,
            transcendentals=16 * group * group,
        ),
        name="attention_backward",
    )(scalars, *pieces, *w_attn, *after, *smalls, qkv, lse)


def expert_weights_kernel(sref, *refs):
    b, refs = refs[:4], refs[4:]
    g, refs = refs[:4], refs[4:]
    dgu, refs = refs[:4], refs[4:]
    ga, refs = refs[:4], refs[4:]
    out_ref, bt_ref, gt_ref = refs
    group = b[0].shape[0]
    dp, _, _, dr, ff = out_ref.shape
    first = sref[1] > 0

    def chosen(four, micro, *index):
        index = index or (Ellipsis,)
        return jnp.where(first, four[micro][index], four[2 + micro][index])

    @pl.when(pl.program_id(0) == 0)
    def _():
        for micro in range(2):
            place = slice(micro * group, (micro + 1) * group)
            bt_ref[:, place] = chosen(b, micro).T
            gt_ref[:, place] = chosen(g, micro).T

    bt = bt_ref[...]
    for j in range(PER):
        rows = jnp.concatenate([chosen(dgu, 0, j), chosen(dgu, 1, j)], axis=0)
        grads = dot(bt, rows).astype(BF)
        out_ref[:, 0, j] = grads[:, :ff].reshape(dp, dr, ff)
        out_ref[:, 1, j] = grads[:, ff:].reshape(dp, dr, ff)
    rows = jnp.concatenate([chosen(ga, 0), chosen(ga, 1)], axis=0)
    grads = dot(gt_ref[...], rows).astype(BF)
    for j in range(PER):
        out_ref[:, 2, j] = grads[:, j * ff : (j + 1) * ff].reshape(dp, dr, ff)


def expert_weights(scalars, rows_b, grads, dgus, gas, dp):
    group, width = rows_b[0].shape
    experts, _, ff2 = dgus[0].shape
    ff = ff2 // 2
    dr = width // dp
    square = whole((group, width))
    wide, flat = [], []
    for held in (lambda s: s[1], lambda s: 1 - s[1]):
        wide += [
            pl.BlockSpec((PER, group, ff2), lambda i, s, held=held: (i * held(s), 0, 0))
        ] * 2
        flat += [pl.BlockSpec((group, PER * ff), lambda i, s, held=held: (0, i * held(s)))] * 2
    return pl.pallas_call(
        expert_weights_kernel,
        grid_spec=pltpu.PrefetchScalarGridSpec(
            num_scalar_prefetch=1,
            grid=(experts // PER,),
            in_specs=[square] * 8 + wide + flat,
            out_specs=pl.BlockSpec((dp, 3, PER, dr, ff), lambda i, s: (0, 0, i, 0, 0)),
            scratch_shapes=[
                pltpu.VMEM((width, 2 * group), BF),
                pltpu.VMEM((width, 2 * group), BF),
            ],
        ),
        out_shape=jax.ShapeDtypeStruct((dp, 3, experts, dr, ff), BF),
        compiler_params=params(),
        cost_estimate=pl.CostEstimate(
            flops=4 * group * width * ff * 3 * experts,
            bytes_accessed=dp * 3 * experts * dr * ff * 2 + 6 * experts * group * ff * 2,
            transcendentals=0,
        ),
        name="expert_weight_grads",
    )(scalars, *rows_b, *grads, *dgus, *gas)


def attention_weights_kernel(sref, *refs):
    a, o, f, d, small = (refs[4 * j : 4 * j + 4] for j in range(5))
    out_ref = refs[20]
    dp = out_ref.shape[0]
    first = sref[1] > 0

    def chosen(four, micro):
        return jnp.where(first, four[micro][...], four[2 + micro][...])

    sums = dot_tn(chosen(a, 0), chosen(d, 0)) + dot_tn(chosen(a, 1), chosen(d, 1))
    for j in range(4):
        out_ref[:, 64 * j : 64 * (j + 1), :] = (
            sums[:, LANES * j : LANES * (j + 1)].astype(BF).reshape(dp, 64, LANES)
        )
    sums = dot_tn(chosen(f, 0), chosen(o, 0)) + dot_tn(chosen(f, 1), chosen(o, 1))
    for j in range(2):
        out_ref[:, 64 * (4 + j) : 64 * (5 + j), :] = (
            sums[:, LANES * j : LANES * (j + 1)].astype(BF).reshape(dp, 64, LANES)
        )
    rows = chosen(small, 0) + chosen(small, 1)
    rows = jnp.concatenate(
        [rows, jnp.zeros((LANES - rows.shape[0], rows.shape[1]), F32)], axis=0
    )
    out_ref[:, 384:, :] = rows.T.astype(BF).reshape(dp, 64, LANES)


def attention_weights(scalars, a, o, f, d, small, dp):
    group, width = a[0].shape
    operands = [*a, *o, *f, *d, *small]
    return pl.pallas_call(
        attention_weights_kernel,
        grid_spec=pltpu.PrefetchScalarGridSpec(
            num_scalar_prefetch=1,
            grid=(1,),
            in_specs=[whole(x.shape) for x in operands],
            out_specs=whole((dp, 448, LANES)),
        ),
        out_shape=jax.ShapeDtypeStruct((dp, 448, LANES), BF),
        compiler_params=params(),
        cost_estimate=pl.CostEstimate(
            flops=4 * group * width * 768,
            bytes_accessed=group * width * 14 + width * 768 * 2,
            transcendentals=0,
        ),
        name="attention_weight_grads",
    )(scalars, *operands)


def moved(array, shift):
    return lax.ppermute(array, "tensor", [(i, (i + shift) % 4) for i in range(4)])


def to_owner(pieces):
    return [pieces[0]] + [moved(pieces[s], s) for s in range(1, 4)]


def to_all(rows):
    return [rows] + [moved(rows, s) for s in range(1, 4)]


def across(rows, up):
    start, end = (0, 4) if up else (4, 0)
    return [
        lax.ppermute(
            rows, ("pipe", "tensor"), [(start + i, end + (i + s) % 4) for i in range(4)]
        )
        for s in range(4)
    ]


def tables_of(lengths, group):
    ends = jnp.cumsum(lengths)
    starts = ends - lengths
    index = jnp.arange(group, dtype=jnp.int32)
    inside = index[:, None] >= starts[None, :]
    start = jnp.max(jnp.where(inside, starts[None, :], 0), axis=1)
    position = (index - start).astype(F32)
    half = HD // 2
    freq = jnp.exp(jnp.arange(half, dtype=F32) * (-2.0 * math.log(10000.0) / HD))
    angle = position[:, None] * freq[None, :]
    cos, sin = jnp.cos(angle), jnp.sin(angle)
    visible = (index[None, :] <= index[:, None]) & (index[None, :] >= start[:, None])
    bias = jnp.where(visible, 0.0, MASKED).astype(F32)
    return (
        jnp.concatenate([cos, cos, cos, cos], axis=1),
        jnp.concatenate([-sin, sin, -sin, sin], axis=1),
        bias,
    )


def per_device(
    inputs, cotangent, doc_lengths, routes, norm_attn, w_query, w_key, w_value, w_out,
    w_router, norm_ffn, w_gate, w_up, w_down,
):
    section = lax.axis_index("pipe")
    first_section = section == 0
    me = lax.axis_index("tensor")
    dp = lax.axis_size("dp")
    micro = inputs.shape[0]
    shard, width = inputs.shape[1:]
    group = shard * 4
    rows_dp = width // dp
    scalars = [
        jnp.stack([me, (section == s).astype(jnp.int32)]).astype(jnp.int32) for s in range(2)
    ]

    out_turned = w_out[0].T
    small = jnp.concatenate([w_router[0], norm_attn[0][:, None], norm_ffn[0][:, None]], axis=1)
    small = jnp.pad(small, ((0, 0), (0, LANES - E - 2)))
    piece = jnp.concatenate(
        [
            w_query[0][:, :LANES], w_query[0][:, LANES:], w_key[0], w_value[0],
            out_turned[:, :LANES], out_turned[:, LANES:], small,
        ],
        axis=0,
    )
    w_own = lax.all_gather(piece, "dp", axis=0)
    pieces_w = jnp.stack([w_gate[0], w_up[0], w_down[0].transpose(0, 2, 1)])
    pieces_w, w_own = lax.optimization_barrier((pieces_w, w_own))
    w_experts = lax.all_gather(pieces_w, "dp", axis=0)
    w_next, w_last = moved(w_own, 1), moved(w_own, 3)
    half = dp // 2
    w_attn = [w_own, w_next, moved(w_next[:half], 1), moved(w_last[half:], 3), w_last]
    router, gains = smalls_of(scalars[0], w_attn)

    rows_in = to_all(inputs)
    rows_in = [[part[m] for part in rows_in] for m in range(micro)]
    rows_cot = to_all(cotangent)
    rows_cot = [[part[m] for part in rows_cot] for m in range(micro)]
    tables = [tables_of(doc_lengths[m, 0], group) for m in range(micro)]
    ids = jnp.arange(E, dtype=jnp.int32)
    picked = jnp.any(routes[0][..., None] == ids, axis=2).astype(F32)

    outputs, saves = [], []
    entering, after = rows_in, []
    for s in range(2):
        kept, sent = [], []
        for m in range(micro):
            (a, xown, qkv, mixed, lse, hown, b, gates) = attention_forward(
                scalars[s], entering[m], gains, tables[m], picked[m], w_attn, router, after
            )
            if m > 0:
                sent.append(finish(parts, hown_before))
            *parts, gu = experts_forward(
                scalars[s], b, gates, w_experts, [sent[-1]] if m > 0 else []
            )
            parts = to_owner(parts)
            hown_before = hown
            after = [gu]
            kept.append((a, xown, qkv, mixed, lse, hown, b, gates, gu))
            if m > 0 and s == 0:
                received = [across(sent[0], True)]
        sent.append(finish(parts, hown_before))
        if s == 0:
            received.append(across(sent[1], True))
            entering = received
        outputs.append(sent)
        saves.append(kept)

    given, own = rows_cot, [cotangent[m] for m in range(micro)]
    grads_in, results = [None, None], [None, None]
    for s in (1, 0):
        kept = saves[s]
        firsts = []
        for m in range(micro):
            gates, gu = kept[m][7], kept[m][8]
            *parts, grad, dgu, ga = experts_backward(
                scalars[s], given[m], gates, gu, w_experts, after
            )
            after = [grad]
            firsts.append((to_owner(parts), grad, dgu, ga))
        if s == 0:
            grad_experts = expert_weights(
                scalars[0],
                [saves[j][m][6] for j in range(2) for m in range(micro)],
                [x[1] for x in firsts + results[1][0]],
                [x[2] for x in firsts + results[1][0]],
                [x[3] for x in firsts + results[1][0]],
                dp,
            )
            after = [grad_experts]
        middles = []
        for m in range(micro):
            dh, do, small = middle(
                scalars[s], firsts[m][0], own[m], kept[m][5], kept[m][7], kept[m][6],
                gains, router, after,
            )
            middles.append((dh, to_all(do), small))
            after = [do]
        lasts, dxs = [], []
        for m in range(micro):
            dh, rows_do, small = middles[m]
            dx, dx_low, small, full, dqkv = attention_backward(
                scalars[s], rows_do, dh, kept[m][1], small, gains, tables[m],
                kept[m][2], kept[m][4], w_attn, after,
            )
            after = [dx]
            dxs.append(dx)
            lasts.append((small, full, dqkv))
            if s == 1:
                if m == 0:
                    received = []
                received.append(across(dx_low, False))
        grads_in[s] = dxs
        results[s] = (firsts, lasts)
        if s == 1:
            given, own = received, [pieces[0] for pieces in received]

    expert_sums = lax.psum_scatter(grad_experts, "dp", scatter_dimension=0, tiled=True)[0]
    lasts = results[0][1] + results[1][1]
    grad_attn = attention_weights(
        scalars[0],
        [saves[s][m][0] for s in range(2) for m in range(micro)],
        [saves[s][m][3] for s in range(2) for m in range(micro)],
        [x[1] for x in lasts],
        [x[2] for x in lasts],
        [x[0] for x in lasts],
        dp,
    )
    grad_attn = lax.all_to_all(grad_attn, "dp", 0, 0, tiled=True)
    attn_sums = jnp.sum(grad_attn.astype(F32), axis=0)
    small = attn_sums[384:].reshape(4, 16, LANES)
    small_own = None
    for shift in range(4):
        part = lax.dynamic_index_in_dim(small, (me + shift) % 4, 0, keepdims=False)
        part = moved(part, shift) if shift else part
        small_own = part if small_own is None else small_own + part
    expert_sums = expert_sums.astype(F32)
    blocks = [attn_sums[64 * j : 64 * (j + 1)] for j in range(6)]
    section_rows = jnp.stack(
        [jnp.where(first_section, outputs[0][m], outputs[1][m]) for m in range(micro)]
    )
    grad_in = jnp.stack(
        [jnp.where(first_section, grads_in[0][m], grads_in[1][m]) for m in range(micro)]
    )
    return (
        section_rows[None],
        grad_in[None],
        small_own[:, E + 1][None],
        jnp.concatenate(blocks[:2], axis=1)[None],
        blocks[2][None],
        blocks[3][None],
        jnp.concatenate(blocks[4:], axis=1).T[None],
        small_own[:, :E][None],
        small_own[:, E][None],
        expert_sums[0][None],
        expert_sums[1][None],
        expert_sums[2].transpose(0, 2, 1)[None],
    )


def finish(parts, hown):
    result = hown
    for part in parts:
        result = result + part.astype(F32)
    return result.astype(BF)


def solution(mesh):
    in_specs = (
        P(None, ("dp", "tensor"), None),
        P(None, ("dp", "tensor"), None),
        P(None, "dp", None),
        P("pipe", None, "dp", None),
        P("pipe", ("dp", "tensor")),
        P("pipe", "dp", "tensor"),
        P("pipe", "dp", "tensor"),
        P("pipe", "dp", "tensor"),
        P("pipe", "tensor", "dp"),
        P("pipe", ("dp", "tensor"), None),
        P("pipe", ("dp", "tensor")),
        P("pipe", None, "dp", "tensor"),
        P("pipe", None, "dp", "tensor"),
        P("pipe", None, "tensor", "dp"),
    )
    out_specs = (
        P("pipe", None, ("dp", "tensor"), None),
        P("pipe", None, ("dp", "tensor"), None),
        P("pipe", ("dp", "tensor")),
        P("pipe", "dp", "tensor"),
        P("pipe", "dp", "tensor"),
        P("pipe", "dp", "tensor"),
        P("pipe", "tensor", "dp"),
        P("pipe", ("dp", "tensor"), None),
        P("pipe", ("dp", "tensor")),
        P("pipe", None, "dp", "tensor"),
        P("pipe", None, "dp", "tensor"),
        P("pipe", None, "tensor", "dp"),
    )
    return jax.shard_map(
        per_device, mesh=mesh, in_specs=in_specs, out_specs=out_specs, check_vma=False
    )
```

time: 936 us -> 531 us (0.57)
  waiting for transfers between devices: 446 us -> 160 us
  blocking collectives: 156 us -> 0 us
  starting transfers between devices: 66.1 us -> 119 us
  Pallas kernels: 189 us -> 174 us
    unnamed x8 -> x3, waiting for transfers between devices: 256 us -> 0.05 us
    all_gather x2 -> x0, blocking collectives: 156 us -> none  [the longest x1 142 us: per_device(): small = lax.all_gather(small, ('dp', 'tensor'), axis=0, tiled=True)]
    reduce_scatter x1, waiting for transfers between devices: 81.3 us -> 0.01 us  [per_device(): lax.psum_scatter(grad_experts, 'dp', scatter_dimension=0, tiled=True)[0]]
    ppermute x43 -> x65, waiting for transfers between devices: 50.6 us -> 114 us  [the longest x16 60 us: across(): lax.ppermute(rows, ('pipe', 'tensor'), [(start + i, end + (i + s) % 4) fo...]
    reduce_scatter x1 -> x0, waiting for transfers between devices: 58.3 us -> none  [per_device(): lax.psum_scatter(grad_attn, 'dp', scatter_dimension=0, tiled=True)[0]]
    ppermute x43 -> x65, starting transfers between devices: 65.6 us -> 114 us  [the longest x49 73 us: moved(): lax.ppermute(array, 'tensor', [(i, (i + shift) % 4) for i in range(4)])]
    all_gather x3 -> x1, waiting for transfers between devices: 0.02 us -> 33.7 us  [per_device(): w_own = lax.all_gather(piece, 'dp', axis=0)]
    pallas_call x16 -> x22, Pallas kernels: 184 us -> 168 us  [the longest x4 38.4 us: attention_backward(): pl.pallas_call(lambda *refs: attention_backward_kernel(len(after), *refs)...]
  transfers between devices with their start and end apart: 50 -> 69, of which waited for: 26 -> 19; matrix products, arithmetic and copies ran while one was open for 4% -> 6% of each run, Pallas kernels for 9% -> 23%
where the time goes in v2:
time: 531 us; the launch traced here: 521 us
  Pallas kernels  174 us (33%)
  waiting for transfers between devices  160 us (30%)
  starting transfers between devices  119 us (22%)
  local copies, waits for them, and re-layouts  32.9 us (6%)
  other arithmetic  19.9 us (4%)
  between operations  15.2 us (3%)
    ppermute x49, starting transfers between devices, moved(): lax.ppermute(array, 'tensor', [(i, (i + shift) % 4) for i in range(4)])  73 us
    ppermute x16, waiting for transfers between devices, across(): lax.ppermute(rows, ('pipe', 'tensor'), [(start + i, end + (i + s) % 4) fo...  60 us
    ppermute x49, waiting for transfers between devices, moved(): lax.ppermute(array, 'tensor', [(i, (i + shift) % 4) for i in range(4)])  54.3 us
    ppermute x16, starting transfers between devices, across(): lax.ppermute(rows, ('pipe', 'tensor'), [(start + i, end + (i + s) % 4) fo...  41.2 us
    pallas_call x4, Pallas kernels, attention_backward(): pl.pallas_call(lambda *refs: attention_backward_kernel(len(after), *refs)...  38.4 us
    pallas_call x4, Pallas kernels, experts_backward(): pl.pallas_call(lambda *refs: experts_backward_kernel(len(after), *refs),...  35.3 us
    all_gather x1, waiting for transfers between devices, per_device(): w_own = lax.all_gather(piece, 'dp', axis=0)  33.7 us
    pallas_call x4, Pallas kernels, attention_forward(): pl.pallas_call(lambda *refs: attention_forward_kernel(len(after), *refs),...  33.4 us
  transfers between devices with their start and end apart: 69, of which 19 were waited for; matrix products, arithmetic and copies ran while one was open for 6% of the time, Pallas kernels for 23%

profile of v2, /device:TPU:0, one launch (start us, length us, event | category | flops | bytes accessed | tf_op | source)
XLA Modules:
  0.0 520.7 jit_solution(4112922011744339834)
XLA Ops:
  16.7 33.7 %all-gather.5.cloned.1.call-done = bf16[6400,128]{1,0:T(8,128)(2,1)} async-done(((bf16[400,128]{1,0:T(8,128)(2,1)}), bf16[6400,128]{1,0:T(8,128)(2,1)}) %all-gather.5.cloned.1.call-update) | async-done | bytes 1638416 | tf_op jit(solution)/shard_map/all_gather | solution.py:848
  79.4 22.8 %collective-permute-done.3.refs_1_.refs_6_ = bf16[16,400,128]{2,1,0:T(8,128)(2,1)S(1)} collective-permute-done((bf16[16,400,128]{2,1,0:T(8,128)(2,1)}, bf16[16,400,128]{2,1,0:T(8,128)(2,1)S(1)}, u32[]{:S(2)}, u32[]{:S(2)}) %collective-permute-start.3) | collective-permute-done | bytes 1638432 | tf_op jit(solution)/shard_map/ppermute | solution.py:781
  109.3 4.8 collective-permute-done.28
  115.5 15.3 %collective-permute-done.4.refs_2_.refs_7_ = bf16[8,400,128]{2,1,0:T(8,128)(2,1)S(1)} collective-permute-done((bf16[8,400,128]{2,1,0:T(8,128)(2,1)S(1)}, bf16[8,400,128]{2,1,0:T(8,128)(2,1)S(1)}, u32[]{:S(2)}, u32[]{:S(2)}) %collective-permute-start.4) | collective-permute-done | bytes 819232 | tf_op jit(solution)/shard_map/ppermute | solution.py:781
  135.1 13.1 %attention_forward.4 = (bf16[256,1024]{1,0:T(8,128)(2,1)}, bf16[64,1024]{1,0:T(8,128)(2,1)}, bf16[4,256,512]{2,1,0:T(8,128)(2,1)}, bf16[256,256]{1,0:T(8,128)(2,...) custom-call(s32[2]{0:T(128)} %pad_add_fusion.sref.refs_0_, ...), custom_call_target="tpu_custom_call" | custom-call | flops 1879048192 | bytes 9437184 | tf_op jit(solution)/shard_map/attention_forward/pallas_call | solution.py:266
  148.3 11.9 %experts_forward.4 = (bf16[64,1024]{1,0:T(8,128)(2,1)}, bf16[64,1024]{1,0:T(8,128)(2,1)}, bf16[64,1024]{1,0:T(8,128)(2,1)}, bf16[64,1024]{1,0:T(8,128)(2,1)}, bf16[16,256,256]{2,1,0:T(8,128)(2,1)}) custom-call(s32[2]{0:T(128)} %pad_add_fusion.sref.refs_0_, bf16[256,1024]{1,0:T(8,128)(2,1)} %get-tuple-element.130.refs_1_.refs_0_.refs_9_, ...), custom_call_target="tpu_custom_call" | custom-call | flops 3221225472 | bytes 14680064 | tf_op jit(solution)/shard_map/experts_forward/pallas_call | solution.py:339
  163.9 13.2 %attention_forward.5 = (bf16[256,1024]{1,0:T(8,128)(2,1)}, bf16[64,1024]{1,0:T(8,128)(2,1)}, bf16[4,256,512]{2,1,0:T(8,128)(2,1)}, bf16[256,256]{1,0:T(8,128)(2,...) custom-call(s32[2]{0:T(128)} %pad_add_fusion.sref.refs_0_, ...), custom_call_target="tpu_custom_call" | custom-call | flops 1879048192 | bytes 9437184 | tf_op jit(solution)/shard_map/attention_forward/pallas_call | solution.py:266
  182.5 11.9 %experts_forward.5 = (bf16[64,1024]{1,0:T(8,128)(2,1)}, bf16[64,1024]{1,0:T(8,128)(2,1)}, bf16[64,1024]{1,0:T(8,128)(2,1)}, bf16[64,1024]{1,0:T(8,128)(2,1)}, bf16[16,256,256]{2,1,0:T(8,128)(2,1)}) custom-call(s32[2]{0:T(128)} %pad_add_fusion.sref.refs_0_, bf16[64,1024]{1,0:T(8,128)(2,1)} %copy-done.4, ...), custom_call_target="tpu_custom_call" | custom-call | flops 3221225472 | bytes 14680064 | tf_op jit(solution)/shard_map/experts_forward/pallas_call | solution.py:339
  199.5 3.5 attention_forward.6
  210.4 18.1 %collective-permute-start.20 = (bf16[64,1024]{1,0:T(8,128)(2,1)S(1)}, bf16[64,1024]{1,0:T(8,128)(2,1)S(1)}, u32[]{:S(2)}, u32[]{:S(2)}) collective-permute-start(bf16[64,1024]{1,0:T(8,128)(2,1)S(1)} %add_convert_fusion.1), channel_id=1, source_target_pairs={{0,64},{1,65},{2,66},{3,67},{4,68},{5,69},{6,70},{7,71},{8,72},{9,... | collective-permute-start | bytes 393224 | tf_op jit(solution)/shard_map/ppermute | solution.py:795
  240.2 3.6 attention_forward.7
  247.0 3.5 experts_backward.4
  254.3 3.5 experts_backward.5
  266.8 3.5 collective-permute-start.40
  293.9 50.7 %collective-permute-done.42.refs_2_.refs_6_ = bf16[64,1024]{1,0:T(8,128)(2,1)S(1)} collective-permute-done((bf16[64,1024]{1,0:T(8,128)(2,1)}, bf16[64,1024]{1,0:T(8,128)(2,1)S(1)}, u32[]{:S(2)}, u32[]{:S(2)}) %collective-permute-start.42) | collective-permute-done | bytes 131104 | tf_op jit(solution)/shard_map/ppermute | solution.py:795
  351.1 14.2 %experts_backward.6 = (bf16[64,1152]{1,0:T(8,128)(2,1)}, bf16[64,1152]{1,0:T(8,128)(2,1)}, bf16[64,1152]{1,0:T(8,128)(2,1)}, bf16[64,1152]{1,0:T(8,128)(2,1)}, b...) custom-call(s32[2]{0:T(128)} %pad_add_fusion.sref.refs_0_, ...), custom_call_target="tpu_custom_call" | custom-call | flops 3221225472 | bytes 17825792 | tf_op jit(solution)/shard_map/experts_backward/pallas_call | solution.py:439
  371.7 14.2 %experts_backward.7 = (bf16[64,1152]{1,0:T(8,128)(2,1)}, bf16[64,1152]{1,0:T(8,128)(2,1)}, bf16[64,1152]{1,0:T(8,128)(2,1)}, bf16[64,1152]{1,0:T(8,128)(2,1)}, b...) custom-call(s32[2]{0:T(128)} %pad_add_fusion.sref.refs_0_, ...), custom_call_target="tpu_custom_call" | custom-call | flops 3221225472 | bytes 17825792 | tf_op jit(solution)/shard_map/experts_backward/pallas_call | solution.py:439
  385.8 15.5 %expert_weight_grads.1.refs_1_ = bf16[16,3,16,64,128]{4,3,2,1,0:T(8,128)(2,1)} custom-call(s32[2]{0:T(128)} %pad_add_fusion.sref.refs_0_, bf16[256,1024]{1,0:T(8,128)(2,1)} %get-tuple-element.130.refs_1_.refs_0_.refs_9_, bf16[256,1024]{1,0:T(8,128)(2,1)} %get-tuple-element.138.refs_2_.refs_1_.refs_9_, ...), custom_call_target="tpu_custom_call" | custom-call | flops 6442450944 | bytes 18874368 | tf_op jit(solution)/shard_map/expert_weight_grads/pallas_call | solution.py:709
  415.7 4.6 collective-permute-start.53
  431.6 15.8 %attention_backward.6 = (f32[64,1024]{1,0:T(8,128)}, bf16[64,1024]{1,0:T(8,128)(2,1)}, f32[24,1024]{1,0:T(8,128)}, bf16[256,1024]{1,0:T(8,128)(2,1)}, bf16[256,512]{1,0:T(8,128)(2,1)}) custom-call(s32[2]{0:T(128)} %pad_add_fusion.sref.refs_0_, bf16[64,1024]{1,0:T(8,128)(2,1)} %get-tuple-element.202.refs_1_, bf16[64,1024]{1,0:T(8,128)(2,1)} %copy-done.31, ...), custom_call_target="tpu_custom_call" | custom-call | flops 1207959552 | bytes 9437184 | tf_op jit(solution)/shard_map/attention_backward/pallas_call | solution.py:633
  448.2 15.8 %attention_backward.7 = (f32[64,1024]{1,0:T(8,128)}, bf16[64,1024]{1,0:T(8,128)(2,1)}, f32[24,1024]{1,0:T(8,128)}, bf16[256,1024]{1,0:T(8,128)(2,1)}, bf16[256,512]{1,0:T(8,128)(2,1)}) custom-call(s32[2]{0:T(128)} %pad_add_fusion.sref.refs_0_, bf16[64,1024]{1,0:T(8,128)(2,1)} %get-tuple-element.207.refs_10_.refs_1_, bf16[64,1024]{1,0:T(8,128)(2,1)} %copy-done.34, ...), custom_call_target="tpu_custom_call" | custom-call | flops 1207959552 | bytes 9437184 | tf_op jit(solution)/shard_map/attention_backward/pallas_call | solution.py:633
  464.1 6.1 %attention_weight_grads.1 = bf16[16,448,128]{2,1,0:T(8,128)(2,1)} custom-call(s32[2]{0:T(128)} %pad_add_fusion.sref.refs_0_, bf16[256,1024]{1,0:T(8,128)(2,1)} %get-tuple-element.220.refs_0_, bf16[256,1024]{1,0:T(8,128)(2,1)} %get-tuple-element.221.refs_1_, bf16[256,1024]{1,0:T(8,128)(2,1)} %get-tuple-element.222.refs_2_, ...), custom_call_target="tpu_custom_call" | custom-call | flops 805306368 | bytes 5242880 | tf_op jit(solution)/shard_map/attention_weight_grads/pallas_call | solution.py:761
  470.2 4.2 all-to-all-start
  488.2 12.1 %all-to-all-done = bf16[16,448,128]{2,1,0:T(8,128)(2,1)S(1)} async-done(((bf16[16,448,128]{2,1,0:T(8,128)(2,1)}), bf16[16,448,128]{2,1,0:T(8,128)(2,1)S(1)}, u32[]{:S(2)}, u32[]{:S(2)}) %all-to-all-start) | async-done | bytes 1835040 | tf_op jit(solution)/shard_map/all_to_all | solution.py:951
  (330 shorter events, 190.0 us)
Async XLA Ops:
  7.2 43.2 %all-gather.5.cloned.1.call-start = ((), (), s32[]{:S(2)}) async-start(), calls=%async_computation.3 | async-start | bytes 1740800 | tf_op jit(solution)/shard_map/all_gather | solution.py:848
  14.5 133.7 %all-gather.7.cloned.1.call-start = ((), (), s32[]{:S(2)}) async-start(), calls=%async_computation.4 | async-start | bytes 13369344 | tf_op jit(solution)/shard_map/all_gather | solution.py:851
  50.4 460.9 %reduce-scatter.2.cloned.1.call-start = ((), (), s32[]{:S(2)}) async-start(), calls=%async_computation.2 | async-start | bytes 13369344 | tf_op jit(solution)/shard_map/reduce_scatter | solution.py:940
  50.4 24.1 %collective-permute-start = (bf16[2,64,1024]{2,1,0:T(8,128)(2,1)}, bf16[2,64,1024]{2,1,0:T(8,128)(2,1)}, u32[]{:S(2)}, u32[]{:S(2)}) collective-permute-start(bf16[2,64,1024]{2,1,0:T(8,128)(2,1)} %param.14), channel_id=1, source_target_pairs={{0,1},{1,2},{2,3},{3,0},{4,5},{5,6},{6,7},{7,4},{8,9},{9,10},{10,1... | collective-permute-start | bytes 786440 | tf_op jit(solution)/shard_map/ppermute | solution.py:781
  52.0 24.3 %collective-permute-start.1 = (bf16[2,64,1024]{2,1,0:T(8,128)(2,1)}, bf16[2,64,1024]{2,1,0:T(8,128)(2,1)}, u32[]{:S(2)}, u32[]{:S(2)}) collective-permute-start(bf16[2,64,1024]{2,1,0:T(8,128)(2,1)} %param.14), channel_id=1, source_target_pairs={{0,2},{1,3},{2,0},{3,1},{4,6},{5,7},{6,4},{7,5},{8,10},{9,11},{10,... | collective-permute-start | bytes 786440 | tf_op jit(solution)/shard_map/ppermute | solution.py:781
  54.7 49.7 %collective-permute-start.2 = (bf16[2,64,1024]{2,1,0:T(8,128)(2,1)}, bf16[2,64,1024]{2,1,0:T(8,128)(2,1)}, u32[]{:S(2)}, u32[]{:S(2)}) collective-permute-start(bf16[2,64,1024]{2,1,0:T(8,128)(2,1)} %param.14), channel_id=1, source_target_pairs={{0,3},{1,0},{2,1},{3,2},{4,7},{5,4},{6,5},{7,6},{8,11},{9,8},{10,9... | collective-permute-start | bytes 786440 | tf_op jit(solution)/shard_map/ppermute | solution.py:781
  60.8 41.4 %collective-permute-start.3 = (bf16[16,400,128]{2,1,0:T(8,128)(2,1)}, bf16[16,400,128]{2,1,0:T(8,128)(2,1)S(1)}, u32[]{:S(2)}, u32[]{:S(2)}) collective-permute-start(bf16[16,400,128]{2,1,0:T(8,128)(2,1)} %bitcast.18.refs_0_.refs_5_), channel_id=1, source_target_pairs={{0,1},{1,2},{2,3},{3,0},{4,5},{5,6},{6,7},{7,4},{8,9},{9,10},{10,1... | collective-permute-start | bytes 4915208 | tf_op jit(solution)/shard_map/ppermute | solution.py:781
  61.4 42.1 %collective-permute-start.5 = (bf16[16,400,128]{2,1,0:T(8,128)(2,1)}, bf16[16,400,128]{2,1,0:T(8,128)(2,1)S(1)}, u32[]{:S(2)}, u32[]{:S(2)}) collective-permute-start(bf16[16,400,128]{2,1,0:T(8,128)(2,1)} %bitcast.18.refs_0_.refs_5_), channel_id=1, source_target_pairs={{0,3},{1,0},{2,1},{3,2},{4,7},{5,4},{6,5},{7,6},{8,11},{9,8},{10,9... | collective-permute-start | bytes 4915208 | tf_op jit(solution)/shard_map/ppermute | solution.py:781
  74.6 34.0 %collective-permute-start.27 = (bf16[2,64,1024]{2,1,0:T(8,128)(2,1)}, bf16[2,64,1024]{2,1,0:T(8,128)(2,1)S(1)}, u32[]{:S(2)}, u32[]{:S(2)}) collective-permute-start(bf16[2,64,1024]{2,1,0:T(8,128)(2,1)} %param.15), channel_id=1, source_target_pairs={{0,1},{1,2},{2,3},{3,0},{4,5},{5,6},{6,7},{7,4},{8,9},{9,10},{10,1... | collective-permute-start | bytes 786440 | tf_op jit(solution)/shard_map/ppermute | solution.py:781
  76.3 37.8 %collective-permute-start.28 = (bf16[2,64,1024]{2,1,0:T(8,128)(2,1)}, bf16[2,64,1024]{2,1,0:T(8,128)(2,1)S(1)}, u32[]{:S(2)}, u32[]{:S(2)}) collective-permute-start(bf16[2,64,1024]{2,1,0:T(8,128)(2,1)} %param.15), channel_id=1, source_target_pairs={{0,2},{1,3},{2,0},{3,1},{4,6},{5,7},{6,4},{7,5},{8,10},{9,11},{10,... | collective-permute-start | bytes 786440 | tf_op jit(solution)/shard_map/ppermute | solution.py:781
  103.5 27.4 %collective-permute-start.4 = (bf16[8,400,128]{2,1,0:T(8,128)(2,1)S(1)}, bf16[8,400,128]{2,1,0:T(8,128)(2,1)S(1)}, u32[]{:S(2)}, u32[]{:S(2)}) collective-permute-start(bf16[8,400,128]{2,1,0:T(8,128)(2,1)S(1)} %slice.176), channel_id=1, source_target_pairs={{0,1},{1,2},{2,3},{3,0},{4,5},{5,6},{6,7},{7,4},{8,9},{9,10},{10,1... | collective-permute-start | bytes 2457608 | tf_op jit(solution)/shard_map/ppermute | solution.py:781
  104.4 26.5 %collective-permute-start.6 = (bf16[8,400,128]{2,1,0:T(8,128)(2,1)S(1)}, bf16[8,400,128]{2,1,0:T(8,128)(2,1)S(1)}, u32[]{:S(2)}, u32[]{:S(2)}) collective-permute-start(bf16[8,400,128]{2,1,0:T(8,128)(2,1)S(1)} %slice.177), channel_id=1, source_target_pairs={{0,3},{1,0},{2,1},{3,2},{4,7},{5,4},{6,5},{7,6},{8,11},{9,8},{10,9... | collective-permute-start | bytes 2457608 | tf_op jit(solution)/shard_map/ppermute | solution.py:781
  206.3 25.5 %collective-permute-start.16 = (bf16[64,1024]{1,0:T(8,128)(2,1)}, bf16[64,1024]{1,0:T(8,128)(2,1)S(1)}, u32[]{:S(2)}, u32[]{:S(2)}) collective-permute-start(bf16[64,1024]{1,0:T(8,128)(2,1)} %get-tuple-element.147), channel_id=1, source_target_pairs={{0,3},{1,0},{2,1},{3,2},{4,7},{5,4},{6,5},{7,6},{8,11},{9,8},{10,9... | collective-permute-start | bytes 393224 | tf_op jit(solution)/shard_map/ppermute | solution.py:781
  208.9 24.2 %collective-permute-start.15 = (bf16[64,1024]{1,0:T(8,128)(2,1)}, bf16[64,1024]{1,0:T(8,128)(2,1)S(1)}, u32[]{:S(2)}, u32[]{:S(2)}) collective-permute-start(bf16[64,1024]{1,0:T(8,128)(2,1)} %get-tuple-element.146), channel_id=1, source_target_pairs={{0,2},{1,3},{2,0},{3,1},{4,6},{5,7},{6,4},{7,5},{8,10},{9,11},{10,... | collective-permute-start | bytes 393224 | tf_op jit(solution)/shard_map/ppermute | solution.py:781
  210.2 25.9 %collective-permute-start.14 = (bf16[64,1024]{1,0:T(8,128)(2,1)}, bf16[64,1024]{1,0:T(8,128)(2,1)S(1)}, u32[]{:S(2)}, u32[]{:S(2)}) collective-permute-start(bf16[64,1024]{1,0:T(8,128)(2,1)} %get-tuple-element.145), channel_id=1, source_target_pairs={{0,1},{1,2},{2,3},{3,0},{4,5},{5,6},{6,7},{7,4},{8,9},{9,10},{10,1... | collective-permute-start | bytes 393224 | tf_op jit(solution)/shard_map/ppermute | solution.py:781
  210.4 29.0 %collective-permute-start.20 = (bf16[64,1024]{1,0:T(8,128)(2,1)S(1)}, bf16[64,1024]{1,0:T(8,128)(2,1)S(1)}, u32[]{:S(2)}, u32[]{:S(2)}) collective-permute-start(bf16[64,1024]{1,0:T(8,128)(2,1)S(1)} %add_convert_fusion.1), channel_id=1, source_target_pairs={{0,64},{1,65},{2,66},{3,67},{4,68},{5,69},{6,70},{7,71},{8,72},{9,... | collective-permute-start | bytes 393224 | tf_op jit(solution)/shard_map/ppermute | solution.py:795
  283.3 61.3 %collective-permute-start.42 = (bf16[64,1024]{1,0:T(8,128)(2,1)}, bf16[64,1024]{1,0:T(8,128)(2,1)S(1)}, u32[]{:S(2)}, u32[]{:S(2)}) collective-permute-start(bf16[64,1024]{1,0:T(8,128)(2,1)} %get-tuple-element.186), channel_id=1, source_target_pairs={{64,0},{65,1},{66,2},{67,3},{68,4},{69,5},{70,6},{71,7},{72,8},{73... | collective-permute-start | bytes 393224 | tf_op jit(solution)/shard_map/ppermute | solution.py:795
  284.6 61.7 %collective-permute-start.43 = (bf16[64,1024]{1,0:T(8,128)(2,1)}, bf16[64,1024]{1,0:T(8,128)(2,1)S(1)}, u32[]{:S(2)}, u32[]{:S(2)}) collective-permute-start(bf16[64,1024]{1,0:T(8,128)(2,1)} %get-tuple-element.186), channel_id=1, source_target_pairs={{64,1},{65,2},{66,3},{67,0},{68,5},{69,6},{70,7},{71,4},{72,9},{73... | collective-permute-start | bytes 393224 | tf_op jit(solution)/shard_map/ppermute | solution.py:795
  285.9 63.3 %collective-permute-start.44 = (bf16[64,1024]{1,0:T(8,128)(2,1)}, bf16[64,1024]{1,0:T(8,128)(2,1)S(1)}, u32[]{:S(2)}, u32[]{:S(2)}) collective-permute-start(bf16[64,1024]{1,0:T(8,128)(2,1)} %get-tuple-element.186), channel_id=1, source_target_pairs={{64,2},{65,3},{66,0},{67,1},{68,6},{69,7},{70,4},{71,5},{72,10},{7... | collective-permute-start | bytes 393224 | tf_op jit(solution)/shard_map/ppermute | solution.py:795
  287.2 63.3 %collective-permute-start.45 = (bf16[64,1024]{1,0:T(8,128)(2,1)}, bf16[64,1024]{1,0:T(8,128)(2,1)S(1)}, u32[]{:S(2)}, u32[]{:S(2)}) collective-permute-start(bf16[64,1024]{1,0:T(8,128)(2,1)} %get-tuple-element.186), channel_id=1, source_target_pairs={{64,3},{65,0},{66,1},{67,2},{68,7},{69,4},{70,5},{71,6},{72,11},{7... | collective-permute-start | bytes 393224 | tf_op jit(solution)/shard_map/ppermute | solution.py:795
  292.6 73.7 %collective-permute-start.46 = (bf16[64,1024]{1,0:T(8,128)(2,1)}, bf16[64,1024]{1,0:T(8,128)(2,1)S(1)}, u32[]{:S(2)}, u32[]{:S(2)}) collective-permute-start(bf16[64,1024]{1,0:T(8,128)(2,1)} %get-tuple-element.188), channel_id=1, source_target_pairs={{64,0},{65,1},{66,2},{67,3},{68,4},{69,5},{70,6},{71,7},{72,8},{73... | collective-permute-start | bytes 393224 | tf_op jit(solution)/shard_map/ppermute | solution.py:795
  344.6 23.4 %collective-permute-start.47 = (bf16[64,1024]{1,0:T(8,128)(2,1)}, bf16[64,1024]{1,0:T(8,128)(2,1)S(1)}, u32[]{:S(2)}, u32[]{:S(2)}) collective-permute-start(bf16[64,1024]{1,0:T(8,128)(2,1)} %get-tuple-element.188), channel_id=1, source_target_pairs={{64,1},{65,2},{66,3},{67,0},{68,5},{69,6},{70,7},{71,4},{72,9},{73... | collective-permute-start | bytes 393224 | tf_op jit(solution)/shard_map/ppermute | solution.py:795
  346.2 24.7 %collective-permute-start.48 = (bf16[64,1024]{1,0:T(8,128)(2,1)}, bf16[64,1024]{1,0:T(8,128)(2,1)S(1)}, u32[]{:S(2)}, u32[]{:S(2)}) collective-permute-start(bf16[64,1024]{1,0:T(8,128)(2,1)} %get-tuple-element.188), channel_id=1, source_target_pairs={{64,2},{65,3},{66,0},{67,1},{68,6},{69,7},{70,4},{71,5},{72,10},{7... | collective-permute-start | bytes 393224 | tf_op jit(solution)/shard_map/ppermute | solution.py:795
  470.2 30.1 %all-to-all-start = ((bf16[16,448,128]{2,1,0:T(8,128)(2,1)}), bf16[16,448,128]{2,1,0:T(8,128)(2,1)S(1)}, u32[]{:S(2)}, u32[]{:S(2)}) async-start(bf16[16,448,128]{2,1,0:T(8,128)(2,1)} %attention_weight_grads.1), calls=%async_computation | async-start | bytes 3670016 | tf_op jit(solution)/shard_map/all_to_all | solution.py:951
  (111 other events, 979.1 us)
Sparse Core Ops, SparseCore 0:
  14.6 35.6 all-gather.4
  52.1 72.0 all-gather.6
  401.5 90.6 reduce-scatter.1
